TPU v7x, 32 devices: a whole 2x2x4 slice. The times are simulated.
32 devices in a mesh: blk: 8 (over y, x, core), off: 4 (over z).
Axes of the slice: x: 2, y: 2, z: 4, core: 2. Of those that a mesh axis runs over, the one named last changes fastest.
Arguments:
- coefficients: bfloat16 [128, 32, 128], P('blk', 'off'), may hold values from -12 to 12
Outputs:
- smoothed: float32 [128, 32, 128], P(('blk', 'off'))
- log_degree: float32 [128], P(('blk', 'off'))
All inputs are finite; a program needn't handle non-finite values.
Results may differ from a plain program's by a relative error of at most 0.005.
Values may be sent and summed in bfloat16 or wider, within the bound.
No kernel may reach another device: no remote copies, remote signals or barrier semaphores. Data moves between devices by JAX's collectives and lax.ppermute only.
A program may use at most 64 MiB of HBM per device.

v0:
```python
import math

import jax
import jax.numpy as jnp
from jax import lax
from jax.sharding import PartitionSpec as P

epsilon = 1e-06
concentration = 40.0


def shifted(array, axis, by):
    count = lax.axis_size(axis)
    return lax.ppermute(array, axis, [(i, (i + by) % count) for i in range(count)])


def angle_tables(angular):
    half_width = angular // 2
    frequency = jnp.arange(half_width, dtype=jnp.int32)
    shifts = jnp.arange(angular, dtype=jnp.int32)
    product = frequency[:, None] * shifts[None, :] % angular
    phase = product.astype(jnp.float32) * (2.0 * math.pi / angular)
    forward = jnp.concatenate([jnp.cos(phase), -jnp.sin(phase)], axis=0)
    return (forward, forward.T)


def inverse_norms(block_values):
    values = block_values.astype(jnp.float32)
    return lax.rsqrt(jnp.sum(values * values, axis=(1, 2)) + epsilon)


def tile_terms(own_block, own_inverse, other_block, offset, forward, backward):
    row_count = own_block.shape[0]
    half_width = own_block.shape[2] // 2
    highest = lax.Precision.HIGHEST
    other_inverse = inverse_norms(other_block)
    swapped = jnp.concatenate(
        [other_block[:, :, half_width:], other_block[:, :, :half_width]], axis=2
    )
    direct = jnp.einsum("irc,jrc->ijc", own_block, other_block, preferred_element_type=jnp.float32)
    mixed_terms = jnp.einsum("irc,jrc->ijc", own_block, swapped, preferred_element_type=jnp.float32)
    real_part = direct[:, :, :half_width] + direct[:, :, half_width:]
    imag_part = mixed_terms[:, :, half_width:] - mixed_terms[:, :, :half_width]
    cross_spectrum = jnp.concatenate([real_part, imag_part], axis=2).reshape(
        row_count * row_count, -1
    )
    correlation = jnp.dot(
        cross_spectrum, forward, precision=highest, preferred_element_type=jnp.float32
    )
    correlation = correlation.reshape(row_count, row_count, -1)
    cosine = correlation * own_inverse[:, None, None] * other_inverse[None, :, None]
    same_image = jnp.arange(row_count)[:, None] == jnp.arange(row_count)[None, :]
    keep_mask = jnp.where(jnp.logical_and(offset == 0, same_image), 0.0, 1.0).astype(jnp.float32)
    weights = jnp.exp(concentration * cosine) * keep_mask[:, :, None]
    spectral = jnp.dot(
        weights.reshape(row_count * row_count, -1),
        backward,
        precision=highest,
        preferred_element_type=jnp.float32,
    ).reshape(row_count, row_count, -1)
    degree = jnp.sum(spectral[:, :, 0], axis=1)
    rounded = spectral.astype(jnp.bfloat16)
    weight_real = jnp.concatenate([rounded[:, :, :half_width], rounded[:, :, :half_width]], axis=2)
    weight_imag = jnp.concatenate([-rounded[:, :, half_width:], rounded[:, :, half_width:]], axis=2)
    filtered = jnp.einsum(
        "ijc,jrc->irc", weight_real, other_block, preferred_element_type=jnp.float32
    )
    filtered = filtered + jnp.einsum(
        "ijc,jrc->irc", weight_imag, swapped, preferred_element_type=jnp.float32
    )
    return (filtered, degree)


def body(coefficients):
    own_block = lax.all_gather(coefficients, "off", axis=1, tiled=True)
    own_inverse = inverse_norms(own_block)
    row_count, radial, angular = own_block.shape
    forward, backward = angle_tables(angular)
    ranges = lax.axis_size("off")
    per_range = min(8, lax.axis_size("blk") // ranges)
    range_index = lax.axis_index("off")
    range_base = range_index * per_range
    packet = own_block
    packet = shifted(packet, "blk", -(per_range // 2))
    for bit_number in range(ranges.bit_length() - 1):
        moved_packet = shifted(packet, "blk", -(per_range << bit_number))
        chosen = range_index // (1 << bit_number) % 2 == 1
        packet = jnp.where(chosen, moved_packet, packet)
    empty_sum = jnp.zeros((row_count, radial, angular), jnp.float32)
    empty_degree = jnp.zeros((row_count,), jnp.float32)
    centre = range_base + per_range // 2
    lower_block = shifted(packet, "blk", 1)

    def advance_both(step, loop_state):
        filtered, degree, upper_block, lower_part = loop_state
        upper_terms = tile_terms(
            own_block, own_inverse, upper_block, centre + step, forward, backward
        )
        lower_terms = tile_terms(
            own_block, own_inverse, lower_part, centre - 1 - step, forward, backward
        )
        upper_block = shifted(upper_block, "blk", -1)
        lower_part = shifted(lower_part, "blk", 1)
        return (
            filtered + upper_terms[0] + lower_terms[0],
            degree + upper_terms[1] + lower_terms[1],
            upper_block,
            lower_part,
        )

    last_step = per_range // 2 - 1
    filtered, degree, upper_block, lower_block = lax.fori_loop(
        0, last_step, advance_both, (empty_sum, empty_degree, packet, lower_block)
    )
    upper_terms = tile_terms(
        own_block, own_inverse, upper_block, centre + last_step, forward, backward
    )
    lower_terms = tile_terms(
        own_block, own_inverse, lower_block, centre - 1 - last_step, forward, backward
    )
    filtered = filtered + upper_terms[0] + lower_terms[0]
    degree = degree + upper_terms[1] + lower_terms[1]
    totals = (
        lax.psum_scatter(filtered, "off", scatter_dimension=0, tiled=True),
        lax.psum_scatter(degree, "off", scatter_dimension=0, tiled=True),
    )
    smoothed = totals[0] / totals[1][:, None, None]
    return (smoothed, jnp.log(totals[1]))


def solution(mesh):
    return jax.shard_map(
        body,
        mesh=mesh,
        in_specs=(P("blk", "off", None),),
        out_specs=(P(("blk", "off"), None, None), P(("blk", "off"))),
        check_vma=False,
    )
```

profile of v0, /device:TPU:0, one launch (start us, length us, event | category | flops | bytes accessed | tf_op | source)
XLA Modules:
  0.0 91.2 jit_solution(6162711789580707457)
XLA Ops:
  7.2 0.0 reduce-scatter.2.cloned.1.call-start
  7.2 1.0 %copy.17 = bf16[16,8,128]{0,1,2:T(8,128)(2,1)S(1)} copy(bf16[16,8,128]{2,1,0:T(8,128)(2,1)} %param.1) | data formatting | bytes 65536 | tf_op args[0]
  8.2 23.4 %all_gather.3 = bf16[16,32,128]{0,1,2:T(8,128)(2,1)S(1)} all-gather(bf16[16,8,128]{0,1,2:T(8,128)(2,1)S(1)} %copy.17), channel_id=1, replica_groups=mesh['blk'=8,'off'=4] {'off'}, dimensions={1}, use_global_device_ids=true | all-gather | bytes 163840 | tf_op jit(solution)/shard_map/all_gather | solution.py:75
  31.6 1.2 %copy.18 = bf16[16,32,128]{2,1,0:T(8,128)(2,1)S(1)} copy(bf16[16,32,128]{0,1,2:T(8,128)(2,1)S(1)} %all_gather.3) | data formatting | bytes 262144 | tf_op jit(solution)/shard_map/all_gather | solution.py:75
  32.8 1.2 %collective-permute-start = (bf16[16,32,128]{2,1,0:T(8,128)(2,1)S(1)}, bf16[16,32,128]{2,1,0:T(8,128)(2,1)S(1)}, u32[]{:S(2)}, u32[]{:S(2)}) collective-permute-start(bf16[16,32,128]{2,1,0:T(8,128)(2,1)S(1)} %copy.18), channel_id=1, source_target_pairs={{0,28},{4,0},{8,4},{12,8},{16,12},{20,16},{24,20},{28,24},{1,29},{... | collective-permute-start | bytes 393224 | tf_op jit(solution)/shard_map/ppermute | solution.py:14
  34.0 0.6 multiply_reduce_fusion
  34.5 2.0 %collective-permute-done = bf16[16,32,128]{2,1,0:T(8,128)(2,1)S(1)} collective-permute-done((bf16[16,32,128]{2,1,0:T(8,128)(2,1)S(1)}, bf16[16,32,128]{2,1,0:T(8,128)(2,1)S(1)}, u32[]{:S(2)}, u32[]{:S(2)}) %collective-permute-start) | collective-permute-done | bytes 131104 | tf_op jit(solution)/shard_map/ppermute | solution.py:14
  36.5 1.3 %collective-permute-start.1 = (bf16[16,32,128]{2,1,0:T(8,128)(2,1)S(1)}, bf16[16,32,128]{2,1,0:T(8,128)(2,1)S(1)}, u32[]{:S(2)}, u32[]{:S(2)}) collective-permute-start(bf16[16,32,128]{2,1,0:T(8,128)(2,1)S(1)} %collective-permute-done), channel_id=1, source_target_pairs={{0,24},{4,28},{8,0},{12,4},{16,8},{20,12},{24,16},{28,20},{1,25},{... | collective-permute-start | bytes 393224 | tf_op jit(solution)/shard_map/ppermute | solution.py:14
  37.9 4.7 %collective-permute-done.1 = bf16[16,32,128]{2,1,0:T(8,128)(2,1)S(1)} collective-permute-done((bf16[16,32,128]{2,1,0:T(8,128)(2,1)S(1)}, bf16[16,32,128]{2,1,0:T(8,128)(2,1)S(1)}, u32[]{:S(2)}, u32[]{:S(2)}) %collective-permute-start.1) | collective-permute-done | bytes 131104 | tf_op jit(solution)/shard_map/ppermute | solution.py:14
  42.5 0.3 collective-permute-start.2
  42.9 0.1 sine_negate_fusion
  43.0 4.8 %collective-permute-done.2 = bf16[16,32,128]{2,1,0:T(8,128)(2,1)S(1)} collective-permute-done((bf16[16,32,128]{2,1,0:T(8,128)(2,1)S(1)}, bf16[16,32,128]{2,1,0:T(8,128)(2,1)S(1)}, u32[]{:S(2)}, u32[]{:S(2)}) %collective-permute-start.2) | collective-permute-done | bytes 131104 | tf_op jit(solution)/shard_map/ppermute | solution.py:14
  47.8 0.2 multiply_reduce_fusion.2
  48.0 0.2 collective-permute-start.3
  48.2 0.1 fusion.34
  48.3 0.4 copy.23
  48.8 0.1 pad_maximum_fusion
  48.9 0.4 copy.20
  49.3 0.4 convolution_bitcast_fusion.2
  49.7 0.1 slice_subtract_fusion.1
  49.8 0.3 copy.22
  50.1 0.4 convolution_bitcast_fusion.3
  50.5 0.1 slice_add_fusion.1
  50.6 0.3 copy.21
  50.9 0.3 fusion.5
  51.2 0.3 fusion.39
  51.5 0.1 fusion.36
  51.6 0.1 pad_maximum_fusion.3
  51.7 0.4 copy.26
  52.1 1.4 %fusion.40 = f32[128,32,16]{1,2,0:T(8,128)} fusion(bf16[16,16,128]{1,0,2:T(8,128)(2,1)S(1)} %copy.26, bf16[16,32,128]{1,0,2:T(8,128)(2,1)S(1)} %copy.20), kind=kOutput, calls=%fused_computation.77 | convolution fusion | flops 2097152 | bytes 458752 | tf_op jit(solution)/shard_map/ijc,jrc->irc/dot_general | solution.py:68
  53.5 0.1 pad_maximum_fusion.2
  53.6 1.2 %copy.24 = bf16[16,16,128]{1,0,2:T(8,128)(2,1)} copy(bf16[16,16,128]{2,1,0:T(8,128)(2,1)S(1)} %pad_maximum_fusion.2) | data formatting | bytes 131072 | tf_op jit(solution)/shard_map/concatenate | solution.py:63
  54.8 0.1 fusion.35
  54.9 0.1 pad_maximum_fusion.1
  55.1 0.4 copy.28
  55.5 0.4 convolution_bitcast_fusion
  55.9 0.1 slice_subtract_fusion
  56.0 0.3 copy.30
  56.3 0.4 copy.31
  56.7 0.4 convolution_bitcast_fusion.1
  57.1 0.1 slice_add_fusion
  57.2 0.3 copy.29
  57.5 0.2 multiply_reduce_fusion.1
  57.7 0.3 fusion.9
  58.0 0.3 fusion.38
  58.3 0.1 fusion.37
  58.4 0.1 pad_maximum_fusion.5
  58.5 0.4 copy.34
  58.9 0.4 fusion.41
  59.3 0.1 pad_maximum_fusion.4
  59.4 0.4 copy.32
  59.9 0.4 convolution_add_fusion
  60.3 0.8 copy-done
  61.1 0.1 copy-done.1
  61.2 0.4 fusion.1
  61.6 1.1 %copy.35 = f32[16,32,128]{2,1,0:T(8,128)} copy(f32[16,32,128]{1,0,2:T(8,128)S(1)} %fusion.1) | data formatting | bytes 524288 | tf_op jit(solution)/shard_map/add | solution.py:121
  62.7 0.0 reduce-scatter.2.cloned.1.call-update
  62.8 0.6 dynamic-slice
  64.0 0.2 slice_reduce_fusion.1
  64.2 0.2 slice_reduce_fusion
  64.4 10.6 %all-reduce = f32[16]{0:T(128)S(1)} all-reduce(f32[16]{0:T(128)S(1)} %add.84), channel_id=3, replica_groups=mesh['blk'=8,'off'=4] {'off'}, use_global_device_ids=true, to_apply=%region_6.7.clone | all-reduce | flops 16 | bytes 128
  75.0 0.6 fusion.33
  75.6 7.2 %reduce-scatter.2.cloned.1.call-done = f32[4,32,128]{2,1,0:T(8,128)} async-done(((f32[16,32,128]{2,1,0:T(8,128)}), f32[4,32,128]{2,1,0:T(8,128)}) %reduce-scatter.2.cloned.1.call-update) | async-done | bytes 65552 | tf_op jit(solution)/shard_map/reduce_scatter | solution.py:124
  82.8 1.5 %broadcast_divide_fusion = f32[4,32,128]{2,1,0:T(8,128)} fusion(f32[4,32,128]{2,1,0:T(8,128)} %reduce-scatter.2.cloned.1.call-done, f32[4]{0:T(128)S(1)} %get-tuple-element.5), kind=kLoop, calls=%fused_computation.48 | loop fusion | flops 16384 | bytes 131088 | tf_op jit(solution)/shard_map/div | solution.py:127
  (12 shorter events, 0.1 us)
Async XLA Ops:
  7.2 75.7 %reduce-scatter.2.cloned.1.call-start = ((), (), s32[]{:S(2)}) async-start(), calls=%async_computation.1 | async-start | bytes 327680 | tf_op jit(solution)/shard_map/reduce_scatter | solution.py:124
  32.8 3.7 %collective-permute-start = (bf16[16,32,128]{2,1,0:T(8,128)(2,1)S(1)}, bf16[16,32,128]{2,1,0:T(8,128)(2,1)S(1)}, u32[]{:S(2)}, u32[]{:S(2)}) collective-permute-start(bf16[16,32,128]{2,1,0:T(8,128)(2,1)S(1)} %copy.18), channel_id=1, source_target_pairs={{0,28},{4,0},{8,4},{12,8},{16,12},{20,16},{24,20},{28,24},{1,29},{... | collective-permute-start | bytes 393224 | tf_op jit(solution)/shard_map/ppermute | solution.py:14
  36.5 6.0 %collective-permute-start.1 = (bf16[16,32,128]{2,1,0:T(8,128)(2,1)S(1)}, bf16[16,32,128]{2,1,0:T(8,128)(2,1)S(1)}, u32[]{:S(2)}, u32[]{:S(2)}) collective-permute-start(bf16[16,32,128]{2,1,0:T(8,128)(2,1)S(1)} %collective-permute-done), channel_id=1, source_target_pairs={{0,24},{4,28},{8,0},{12,4},{16,8},{20,12},{24,16},{28,20},{1,25},{... | collective-permute-start | bytes 393224 | tf_op jit(solution)/shard_map/ppermute | solution.py:14
  42.5 5.2 %collective-permute-start.2 = (bf16[16,32,128]{2,1,0:T(8,128)(2,1)S(1)}, bf16[16,32,128]{2,1,0:T(8,128)(2,1)S(1)}, u32[]{:S(2)}, u32[]{:S(2)}) collective-permute-start(bf16[16,32,128]{2,1,0:T(8,128)(2,1)S(1)} %broadcast_select_fusion), channel_id=1, source_target_pairs={{0,16},{4,20},{8,24},{12,28},{16,0},{20,4},{24,8},{28,12},{1,17},{... | collective-permute-start | bytes 393224 | tf_op jit(solution)/shard_map/ppermute | solution.py:14
  48.0 6.8 %collective-permute-start.3 = (bf16[16,32,128]{2,1,0:T(8,128)(2,1)S(1)}, bf16[16,32,128]{2,1,0:T(8,128)(2,1)S(1)}, u32[]{:S(2)}, u32[]{:S(2)}) collective-permute-start(bf16[16,32,128]{2,1,0:T(8,128)(2,1)S(1)} %get-tuple-element.7), channel_id=1, source_target_pairs={{0,4},{4,8},{8,12},{12,16},{16,20},{20,24},{24,28},{28,0},{1,5},{5... | collective-permute-start | bytes 393224 | tf_op jit(solution)/shard_map/ppermute | solution.py:14
  59.9 1.2 %copy-start = (f32[128,32,16]{1,2,0:T(8,128)S(1)}, f32[128,32,16]{1,2,0:T(8,128)}, u32[]{:S(2)}) copy-start(f32[128,32,16]{1,2,0:T(8,128)} %fusion.40) | copy-start | bytes 786436
  59.9 1.3 %copy-start.1 = (bf16[16,16,128]{1,0,2:T(8,128)(2,1)S(1)}, bf16[16,16,128]{1,0,2:T(8,128)(2,1)}, u32[]{:S(2)}) copy-start(bf16[16,16,128]{1,0,2:T(8,128)(2,1)} %copy.24) | copy-start | bytes 196612
  61.6 1.2 %copy-start.2 = (u32[32]{0:T(128)S(1)}, u32[32]{0:T(128)}, u32[]{:S(2)}) copy-start(u32[32]{0:T(128)} %constant.70) | copy-start | bytes 388
Sparse Core Ops, SparseCore 0:
  62.9 19.8 reduce-scatter.1
where the time goes:
time: 91.5 us; the launch traced here: 91.2 us
  blocking collectives  34 us (37%)
  waiting for transfers between devices  18.7 us (20%)
  between operations  15 us (16%)
  local copies, waits for them, and re-layouts  10.9 us (12%)
  matrix products  5.46 us (6%)
  other arithmetic  4.18 us (5%)
  starting transfers between devices  3.05 us (3%)
    all_gather x1, blocking collectives, body(): own_block = lax.all_gather(coefficients, 'off', axis=1, tiled=True)  23.4 us
    ppermute x4, waiting for transfers between devices, shifted(): lax.ppermute(array, axis, [(i, (i + by) % count) for i in range(count)])  11.4 us
    unnamed x1, blocking collectives  10.6 us
    reduce_scatter x1, waiting for transfers between devices, body(): lax.psum_scatter(filtered, 'off', scatter_dimension=0, tiled=True)  7.22 us
    ppermute x4, starting transfers between devices, shifted(): lax.ppermute(array, axis, [(i, (i + by) % count) for i in range(count)])  3.02 us
    unnamed x8, local copies, waits for them, and re-layouts  2.54 us
  transfers between devices with their start and end apart: 5, of which 4 were waited for; matrix products, arithmetic and copies ran while one was open for 10% of the time, Pallas kernels for 0%

commit v1 on v0

v1 whole, which is shorter than its diff:
```python
import functools
import math

import jax
import jax.numpy as jnp
import numpy as np
from jax import lax
from jax.experimental import pallas as pl
from jax.experimental.pallas import tpu as pltpu
from jax.sharding import PartitionSpec as P

epsilon = 1e-06
concentration = 40.0


def angle_tables(angular):
    half = angular // 2
    product = np.outer(np.arange(half), np.arange(angular)) % angular
    phase = product.astype(np.float32) * np.float32(2.0 * math.pi / angular)
    real, imag = np.cos(phase), -np.sin(phase)
    forward = np.concatenate([real, real, imag, -imag], axis=0)
    backward = np.concatenate([real, real, imag, -imag], axis=0).T
    return forward.astype(np.float32), np.ascontiguousarray(backward).astype(np.float32)


def is_power_of_two(n):
    return n & (n - 1) == 0


def moved(array, axis, pairs):
    return lax.ppermute(array, axis, pairs)


def flipped(array, axis, by):
    return moved(array, axis, [(i, i ^ by) for i in range(lax.axis_size(axis))])


def shifted(array, axis, by):
    count = lax.axis_size(axis)
    return moved(array, axis, [(i, (i + by) % count) for i in range(count)])


def slice_owner(position, step, count):
    if is_power_of_two(count):
        return position ^ step
    return (position + step) % count


def radial_slices(local):
    count = lax.axis_size("off")
    if is_power_of_two(count):
        return [local] + [flipped(local, "off", k) for k in range(1, count)]
    return [local] + [shifted(local, "off", -k) for k in range(1, count)]


def assemble_kernel(*refs):
    *slices, out, wide = refs
    images, depth, angular = slices[0].shape
    for k, piece in enumerate(slices):
        wide[...] = piece[...].astype(jnp.float32).reshape(images * depth, angular)
        for r in range(depth):
            rows = wide[pl.ds(r, images, stride=depth), :]
            out[k * depth + r] = rows.astype(out.dtype)


def assemble(slices):
    images, depth, angular = slices[0].shape
    vmem = pl.BlockSpec(memory_space=pltpu.VMEM)
    return pl.pallas_call(
        assemble_kernel,
        out_shape=jax.ShapeDtypeStruct((len(slices) * depth, images, angular), slices[0].dtype),
        in_specs=[vmem] * len(slices),
        out_specs=vmem,
        scratch_shapes=[pltpu.VMEM((images * depth, angular), jnp.float32)],
        name="assemble",
    )(*slices)


def window_blocks(column):
    count = lax.axis_size("blk")
    ranges = lax.axis_size("off")
    window = ranges * min(8, count // ranges)
    if window == count and is_power_of_two(count):
        groups = [column]
        bits = [1 << b for b in range(1, count.bit_length() - 1)]
        while bits:
            pair, bits = bits[:2], bits[2:]
            flips = [pair[0]] if len(pair) == 1 else [pair[0], pair[1], pair[0] | pair[1]]
            groups = groups + [flipped(g, "blk", f) for f in flips for g in groups]
        if count > 1:
            groups = groups + [flipped(g, "blk", 1) for g in groups]
        return [g[None] for g in groups]
    group = column[None]
    while group.shape[0] < window:
        held = group.shape[0]
        group = jnp.concatenate(
            [group, shifted(group[: min(held, window - held)], "blk", -held)], axis=0
        )
    return [group]


def filter_kernel(ranges, forward, backward, *refs):
    *groups, out, log_degree, own, direct_own, swapped_own, terms, norms, real_w, imag_w = refs
    _, radial, images, angular = groups[0].shape
    half = angular // 2
    rows = images // ranges
    depth = radial // ranges
    place = lax.axis_index("off")
    first = place * rows
    f32 = jnp.float32
    blocks = sum(g.shape[0] for g in groups)
    partners = blocks * images

    def spread(r, carry):
        own[...] = groups[0][0, r].astype(f32)
        for i in range(rows):
            row = own[pl.ds(first + i, 1), :]
            direct_own[i, r] = jnp.broadcast_to(row, (8, angular))
            swapped_own[i, r] = jnp.broadcast_to(pltpu.roll(row, half, 1), (8, angular))
        return carry

    lax.fori_loop(0, radial, spread, 0)

    def cross(group, b, start):
        def step(r, carry):
            direct, mixed, square = carry
            direct, mixed = list(direct), list(mixed)
            x = group[b, r].astype(f32).reshape(images // 8, 8, angular)
            for i in range(rows):
                direct[i] = direct[i] + direct_own[i, r][None] * x
                mixed[i] = mixed[i] + swapped_own[i, r][None] * x
            return tuple(direct), tuple(mixed), square + x * x

        zero = jnp.zeros((images // 8, 8, angular), f32)
        direct, mixed, square = lax.fori_loop(
            0, radial, step, ((zero,) * rows, (zero,) * rows, zero), unroll=4
        )
        for i in range(rows):
            at = pl.ds(i * partners + start, images)
            terms[at, :angular] = direct[i].reshape(images, angular)
            terms[at, angular:] = mixed[i].reshape(images, angular)
        norms[pl.ds(start, images), :] = square.reshape(images, angular)

    start = 0
    for group in groups:
        count = group.shape[0]
        if count == 1:
            cross(group, 0, start)
        else:

            def one(b, carry, group=group, start=start):
                cross(group, b, pl.multiple_of(start + b * images, images))
                return carry

            lax.fori_loop(0, count, one, 0)
        start += count * images

    highest = lax.Precision.HIGHEST
    correlation = jnp.dot(terms[...], forward[...], precision=highest, preferred_element_type=f32)
    inverse = lax.rsqrt(jnp.sum(norms[...], axis=1, keepdims=True) + epsilon)
    numbers = lax.broadcasted_iota(jnp.int32, (partners, angular), 0)
    weights = []
    for i in range(rows):
        mine = direct_own[i, :, 0, :]
        own_inverse = lax.rsqrt(jnp.sum(mine * mine, keepdims=True) + epsilon)
        cosine = correlation[i * partners : (i + 1) * partners] * own_inverse * inverse
        weights.append(jnp.where(numbers == first + i, 0.0, jnp.exp(concentration * cosine)))
    spectral = jnp.dot(
        jnp.concatenate(weights, axis=0), backward[...], precision=highest, preferred_element_type=f32
    )
    scales = []
    logs = []
    for i in range(rows):
        part = spectral[i * partners : (i + 1) * partners]
        degree = jnp.sum(part[:, :angular], axis=0, keepdims=True)[:, :1]
        scales.append(1.0 / degree)
        logs.append(jnp.log(degree))
        real_w[i] = part[:, :angular].astype(jnp.bfloat16).astype(f32)
        imag_w[i] = part[:, angular:].astype(jnp.bfloat16).astype(f32)
    log_degree[...] = jnp.broadcast_to(jnp.concatenate(logs, axis=0), (rows, angular))

    def filtered(pair, carry):
        pair_rows = (2 * pair, 2 * pair + 1)
        zero = jnp.zeros((8, angular), f32)
        sums = ((zero,) * rows, (zero,) * rows), ((zero,) * rows, (zero,) * rows)

        def accumulate(group, b, start, sums):
            new = [(list(s[0]), list(s[1])) for s in sums]
            xs = [group[b, r].astype(f32) for r in pair_rows]
            for v in range(images // 8):
                for i in range(rows):
                    real = real_w[i, pl.ds(start + 8 * v, 8), :]
                    imag = imag_w[i, pl.ds(start + 8 * v, 8), :]
                    for n in range(2):
                        x = xs[n][8 * v : 8 * v + 8]
                        new[n][0][i] = new[n][0][i] + real * x
                        new[n][1][i] = new[n][1][i] + imag * x
            return tuple((tuple(a), tuple(b)) for a, b in new)

        start = 0
        for group in groups:
            count = group.shape[0]
            if count == 1:
                sums = accumulate(group, 0, start, sums)
            else:
                sums = lax.fori_loop(
                    0,
                    count,
                    lambda b, s, group=group, start=start: accumulate(
                        group, b, pl.multiple_of(start + b * images, images), s
                    ),
                    sums,
                )
            start += count * images
        for n in range(2):
            r = pair_rows[n]
            target = slice_owner(place, r // depth, ranges) * depth + r % depth
            for i in range(rows):
                real = jnp.sum(sums[n][0][i], axis=0, keepdims=True)
                imag = jnp.sum(sums[n][1][i], axis=0, keepdims=True)
                out[i, pl.ds(target, 1), :] = (real + pltpu.roll(imag, half, 1)) * scales[i]
        return carry

    lax.fori_loop(0, radial // 2, filtered, 0)


def filter_images(groups, ranges):
    _, radial, images, angular = groups[0].shape
    rows = images // ranges
    partners = images * sum(g.shape[0] for g in groups)
    forward, backward = angle_tables(angular)
    vmem = pl.BlockSpec(memory_space=pltpu.VMEM)
    f32 = jnp.float32
    return pl.pallas_call(
        functools.partial(filter_kernel, ranges),
        out_shape=(
            jax.ShapeDtypeStruct((rows, radial, angular), f32),
            jax.ShapeDtypeStruct((rows, angular), f32),
        ),
        in_specs=[vmem] * (2 + len(groups)),
        out_specs=(vmem, vmem),
        scratch_shapes=[
            pltpu.VMEM((images, angular), f32),
            pltpu.VMEM((rows, radial, 8, angular), f32),
            pltpu.VMEM((rows, radial, 8, angular), f32),
            pltpu.VMEM((rows * partners, 2 * angular), f32),
            pltpu.VMEM((partners, angular), f32),
            pltpu.VMEM((rows, partners, angular), f32),
            pltpu.VMEM((rows, partners, angular), f32),
        ],
        compiler_params=pltpu.CompilerParams(vmem_limit_bytes=48 * 1024 * 1024),
        name="filter",
    )(forward, backward, *groups)


def body(coefficients):
    ranges = lax.axis_size("off")
    column = assemble(radial_slices(coefficients))
    smoothed, log_degree = filter_images(window_blocks(column), ranges)
    return smoothed, log_degree[:, 0]


def solution(mesh):
    return jax.shard_map(
        body,
        mesh=mesh,
        in_specs=(P("blk", "off", None),),
        out_specs=(P(("blk", "off"), None, None), P(("blk", "off"))),
        check_vma=False,
    )
```

time: 91.5 us -> 34.7 us (0.38)
  blocking collectives: 34 us -> 0 us
  between operations: 15 us -> 0.66 us
  Pallas kernels: 0 us -> 10.3 us
  local copies, waits for them, and re-layouts: 10.9 us -> 2.17 us
  waiting for transfers between devices: 18.7 us -> 11.7 us
  starting transfers between devices: 3.05 us -> 9.68 us
  matrix products: 5.46 us -> 0 us
  other arithmetic: 4.18 us -> 0 us
    all_gather x1 -> x0, blocking collectives: 23.4 us -> none  [body(): own_block = lax.all_gather(coefficients, 'off', axis=1, tiled=True)]
    unnamed x1 -> x0, blocking collectives: 10.6 us -> none
    pallas_call x0 -> x2, Pallas kernels: none -> 10.3 us  [the longest x1 8.74 us: filter_images(): pl.pallas_call(functools.partial(filter_kernel, ranges), out_shape=(jax.S...]
    reduce_scatter x1 -> x0, waiting for transfers between devices: 7.22 us -> none  [body(): lax.psum_scatter(filtered, 'off', scatter_dimension=0, tiled=True)]
    ppermute x4 -> x10, starting transfers between devices: 3.02 us -> 9.68 us  [moved(): return lax.ppermute(array, axis, pairs)]
    dot_general x12 -> x0, matrix products: 5.46 us -> none  [the longest x2 1.79 us: tile_terms(): jnp.einsum('ijc,jrc->irc', weight_imag, swapped, preferred_element_type=j...]
    concatenate x6 -> x0, local copies, waits for them, and re-layouts: 3.35 us -> none  [the longest x2 1.64 us: tile_terms(): jnp.concatenate([rounded[:, :, :half_width], rounded[:, :, :half_width]],...]
    add x3 -> x0, local copies, waits for them, and re-layouts: 1.65 us -> none  [the longest x1 1.11 us: body(): filtered = filtered + upper_terms[0] + lower_terms[0]]
  transfers between devices with their start and end apart: 5 -> 10, of which waited for: 4 -> 7; matrix products, arithmetic and copies ran while one was open for 10% -> 0% of each run, Pallas kernels for 0% -> 0%
where the time goes in v1:
time: 34.7 us; the launch traced here: 34.5 us
  waiting for transfers between devices  11.7 us (34%)
  Pallas kernels  10.3 us (30%)
  starting transfers between devices  9.68 us (28%)
  local copies, waits for them, and re-layouts  2.17 us (6%)
  between operations  0.66 us (2%)
    ppermute x10, waiting for transfers between devices, moved(): return lax.ppermute(array, axis, pairs)  11.7 us
    ppermute x10, starting transfers between devices, moved(): return lax.ppermute(array, axis, pairs)  9.68 us
    pallas_call x1, Pallas kernels, filter_images(): pl.pallas_call(functools.partial(filter_kernel, ranges), out_shape=(jax.S...  8.74 us
    unnamed x12, local copies, waits for them, and re-layouts  1.55 us
    pallas_call x1, Pallas kernels, assemble(): pl.pallas_call(assemble_kernel, out_shape=jax.ShapeDtypeStruct((len(slice...  1.52 us
  transfers between devices with their start and end apart: 10, of which 7 were waited for; matrix products, arithmetic and copies ran while one was open for 0% of the time, Pallas kernels for 0%

profile of v1, /device:TPU:0, one launch (start us, length us, event | category | flops | bytes accessed | tf_op | source)
XLA Modules:
  0.0 34.5 jit_solution(18063173623388756484)
XLA Ops:
  0.6 0.0 copy-start.1
  0.6 0.0 copy-start.2
  0.7 4.1 %collective-permute-start.1 = (bf16[16,8,128]{2,1,0:T(8,128)(2,1)}, bf16[16,8,128]{2,1,0:T(8,128)(2,1)S(1)}, u32[]{:S(2)}, u32[]{:S(2)}) collective-permute-start(bf16[16,8,128]{2,1,0:T(8,128)(2,1)} %refs_0_.1), channel_id=1, source_target_pairs={{0,2},{1,3},{2,0},{3,1},{4,6},{5,7},{6,4},{7,5},{8,10},{9,11},{10,... | collective-permute-start | bytes 98312 | tf_op jit(solution)/shard_map/ppermute | solution.py:31
  4.8 1.6 %collective-permute-start = (bf16[16,8,128]{2,1,0:T(8,128)(2,1)}, bf16[16,8,128]{2,1,0:T(8,128)(2,1)S(1)}, u32[]{:S(2)}, u32[]{:S(2)}) collective-permute-start(bf16[16,8,128]{2,1,0:T(8,128)(2,1)} %refs_0_.1), channel_id=1, source_target_pairs={{0,1},{1,0},{2,3},{3,2},{4,5},{5,4},{6,7},{7,6},{8,9},{9,8},{10,11... | collective-permute-start | bytes 98312 | tf_op jit(solution)/shard_map/ppermute | solution.py:31
  6.3 0.0 collective-permute-start.2
  6.3 1.0 %collective-permute-done.1.refs_2_ = bf16[16,8,128]{2,1,0:T(8,128)(2,1)S(1)} collective-permute-done((bf16[16,8,128]{2,1,0:T(8,128)(2,1)}, bf16[16,8,128]{2,1,0:T(8,128)(2,1)S(1)}, u32[]{:S(2)}, u32[]{:S(2)}) %collective-permute-start.1) | collective-permute-done | bytes 32800 | tf_op jit(solution)/shard_map/ppermute | solution.py:31
  7.3 0.0 copy-start.3
  7.3 1.6 %collective-permute-done.refs_1_ = bf16[16,8,128]{2,1,0:T(8,128)(2,1)S(1)} collective-permute-done((bf16[16,8,128]{2,1,0:T(8,128)(2,1)}, bf16[16,8,128]{2,1,0:T(8,128)(2,1)S(1)}, u32[]{:S(2)}, u32[]{:S(2)}) %collective-permute-start) | collective-permute-done | bytes 32800 | tf_op jit(solution)/shard_map/ppermute | solution.py:31
  8.9 0.0 copy-start.4
  8.9 3.4 %collective-permute-done.2.refs_3_ = bf16[16,8,128]{2,1,0:T(8,128)(2,1)S(1)} collective-permute-done((bf16[16,8,128]{2,1,0:T(8,128)(2,1)}, bf16[16,8,128]{2,1,0:T(8,128)(2,1)S(1)}, u32[]{:S(2)}, u32[]{:S(2)}) %collective-permute-start.2) | collective-permute-done | bytes 32800 | tf_op jit(solution)/shard_map/ppermute | solution.py:31
  12.3 0.0 copy-done.3
  12.3 0.0 copy-done.4
  12.3 0.0 copy-start.5
  12.3 0.6 %copy-done.5 = bf16[16,8,128]{2,1,0:T(8,128)(2,1)} copy-done((bf16[16,8,128]{2,1,0:T(8,128)(2,1)}, bf16[16,8,128]{2,1,0:T(8,128)(2,1)S(1)}, u32[]{:S(2)}) %copy-start.5) | copy-done | bytes 32792
  12.9 1.5 %assemble.1 = bf16[32,16,128]{2,1,0:T(8,128)(2,1)} custom-call(bf16[16,8,128]{2,1,0:T(8,128)(2,1)} %refs_0_.1, bf16[16,8,128]{2,1,0:T(8,128)(2,1)} %copy-done.4, bf16[16,8,128]{2,1,0:T(8,128)(2,1)} %copy-done.3, bf16[16,8,128]{2,1,0:T(8,128)(2,1)} %copy-done.5), custom_call_target="tpu_custom_call" | custom-call | tf_op jit(solution)/shard_map/assemble/pallas_call | solution.py:69
  14.4 2.4 %collective-permute-start.5 = (bf16[32,16,128]{2,1,0:T(8,128)(2,1)}, bf16[32,16,128]{2,1,0:T(8,128)(2,1)S(1)}, u32[]{:S(2)}, u32[]{:S(2)}) collective-permute-start(bf16[32,16,128]{2,1,0:T(8,128)(2,1)} %assemble.1), channel_id=1, source_target_pairs={{0,24},{4,28},{8,16},{12,20},{16,8},{20,12},{24,0},{28,4},{1,25},{... | collective-permute-start | bytes 393224 | tf_op jit(solution)/shard_map/ppermute | solution.py:31
  16.9 0.5 %collective-permute-start.4 = (bf16[32,16,128]{2,1,0:T(8,128)(2,1)}, bf16[32,16,128]{2,1,0:T(8,128)(2,1)S(1)}, u32[]{:S(2)}, u32[]{:S(2)}) collective-permute-start(bf16[32,16,128]{2,1,0:T(8,128)(2,1)} %assemble.1), channel_id=1, source_target_pairs={{0,16},{4,20},{8,24},{12,28},{16,0},{20,4},{24,8},{28,12},{1,17},{... | collective-permute-start | bytes 393224 | tf_op jit(solution)/shard_map/ppermute | solution.py:31
  17.4 0.5 %collective-permute-start.3 = (bf16[32,16,128]{2,1,0:T(8,128)(2,1)}, bf16[32,16,128]{2,1,0:T(8,128)(2,1)S(1)}, u32[]{:S(2)}, u32[]{:S(2)}) collective-permute-start(bf16[32,16,128]{2,1,0:T(8,128)(2,1)} %assemble.1), channel_id=1, source_target_pairs={{0,8},{4,12},{8,0},{12,4},{16,24},{20,28},{24,16},{28,20},{1,9},{5... | collective-permute-start | bytes 393224 | tf_op jit(solution)/shard_map/ppermute | solution.py:31
  17.9 0.0 collective-permute-start.6
  17.9 3.8 %collective-permute-done.5 = bf16[32,16,128]{2,1,0:T(8,128)(2,1)S(1)} collective-permute-done((bf16[32,16,128]{2,1,0:T(8,128)(2,1)}, bf16[32,16,128]{2,1,0:T(8,128)(2,1)S(1)}, u32[]{:S(2)}, u32[]{:S(2)}) %collective-permute-start.5) | collective-permute-done | bytes 131104 | tf_op jit(solution)/shard_map/ppermute | solution.py:31
  21.7 0.0 collective-permute-start.9
  21.7 1.0 %collective-permute-done.4 = bf16[32,16,128]{2,1,0:T(8,128)(2,1)S(1)} collective-permute-done((bf16[32,16,128]{2,1,0:T(8,128)(2,1)}, bf16[32,16,128]{2,1,0:T(8,128)(2,1)S(1)}, u32[]{:S(2)}, u32[]{:S(2)}) %collective-permute-start.4) | collective-permute-done | bytes 131104 | tf_op jit(solution)/shard_map/ppermute | solution.py:31
  22.7 0.0 collective-permute-start.8
  22.7 0.0 collective-permute-done.3
  22.7 0.5 %collective-permute-start.7 = (bf16[32,16,128]{2,1,0:T(8,128)(2,1)S(1)}, bf16[32,16,128]{2,1,0:T(8,128)(2,1)S(1)}, u32[]{:S(2)}, u32[]{:S(2)}) collective-permute-start(bf16[32,16,128]{2,1,0:T(8,128)(2,1)S(1)} %collective-permute-done.3), channel_id=1, source_target_pairs={{0,4},{4,0},{8,12},{12,8},{16,20},{20,16},{24,28},{28,24},{1,5},{5... | collective-permute-start | bytes 393224 | tf_op jit(solution)/shard_map/ppermute | solution.py:31
  23.2 0.0 collective-permute-done.6
  23.2 0.0 collective-permute-done.9
  23.2 0.8 %collective-permute-done.8 = bf16[32,16,128]{2,1,0:T(8,128)(2,1)S(1)} collective-permute-done((bf16[32,16,128]{2,1,0:T(8,128)(2,1)S(1)}, bf16[32,16,128]{2,1,0:T(8,128)(2,1)S(1)}, u32[]{:S(2)}, u32[]{:S(2)}) %collective-permute-start.8) | collective-permute-done | bytes 131104 | tf_op jit(solution)/shard_map/ppermute | solution.py:31
  24.0 0.2 collective-permute-done.7
  24.2 0.0 copy-done.1
  24.2 0.0 copy-done.2
  24.2 0.0 copy-start
  24.2 0.9 %copy-done = bf16[32,16,128]{2,1,0:T(8,128)(2,1)S(1)} copy-done((bf16[32,16,128]{2,1,0:T(8,128)(2,1)S(1)}, bf16[32,16,128]{2,1,0:T(8,128)(2,1)}, u32[]{:S(2)}) %copy-start) | copy-done | bytes 131096
  25.1 8.7 %filter.1 = (f32[4,32,128]{2,1,0:T(8,128)}, f32[4,128]{1,0:T(4,128)S(1)}) custom-call(f32[256,128]{1,0:T(8,128)S(1)} %copy-done.2, f32[128,256]{1,0:T(8,128)S(1)} %copy-done.1, bf16[1,32,16,128]{3,2,1,0:T(8,128)(2,1)S(1)} %bitcast.8, bf16[1,32,16,128]{3,2,1,0:T(8,128)(2,1)S(1)} %bitcast.11, bf16[1,32,16,128]{3,2,1,0:T(8,128)(2,1)S(1)} %bitcast.10, ...), custom_call_target="tpu_custom_call" | custom-call | tf_op jit(solution)/shard_map/filter/pallas_call | solution.py:234
  33.9 0.6 %slice_reduce_fusion = f32[4]{0:T(128)} fusion(f32[4,128]{1,0:T(4,128)S(1)} %get-tuple-element.5), kind=kLoop, calls=%fused_computation | loop fusion | bytes 32 | tf_op jit(solution)/shard_map/slice | solution.py:260
Async XLA Ops:
  0.6 23.6 %copy-start.1 = (f32[128,256]{1,0:T(8,128)S(1)}, f32[128,256]{1,0:T(8,128)}, u32[]{:S(2)}) copy-start(f32[128,256]{1,0:T(8,128)} %constant.5.clone.backward) | copy-start | bytes 393220
  0.6 23.6 %copy-start.2 = (f32[256,128]{1,0:T(8,128)S(1)}, f32[256,128]{1,0:T(8,128)}, u32[]{:S(2)}) copy-start(f32[256,128]{1,0:T(8,128)} %constant.4.clone.forward) | copy-start | bytes 393220
  0.7 6.7 %collective-permute-start.1 = (bf16[16,8,128]{2,1,0:T(8,128)(2,1)}, bf16[16,8,128]{2,1,0:T(8,128)(2,1)S(1)}, u32[]{:S(2)}, u32[]{:S(2)}) collective-permute-start(bf16[16,8,128]{2,1,0:T(8,128)(2,1)} %refs_0_.1), channel_id=1, source_target_pairs={{0,2},{1,3},{2,0},{3,1},{4,6},{5,7},{6,4},{7,5},{8,10},{9,11},{10,... | collective-permute-start | bytes 98312 | tf_op jit(solution)/shard_map/ppermute | solution.py:31
  4.8 4.1 %collective-permute-start = (bf16[16,8,128]{2,1,0:T(8,128)(2,1)}, bf16[16,8,128]{2,1,0:T(8,128)(2,1)S(1)}, u32[]{:S(2)}, u32[]{:S(2)}) collective-permute-start(bf16[16,8,128]{2,1,0:T(8,128)(2,1)} %refs_0_.1), channel_id=1, source_target_pairs={{0,1},{1,0},{2,3},{3,2},{4,5},{5,4},{6,7},{7,6},{8,9},{9,8},{10,11... | collective-permute-start | bytes 98312 | tf_op jit(solution)/shard_map/ppermute | solution.py:31
  6.3 5.9 %collective-permute-start.2 = (bf16[16,8,128]{2,1,0:T(8,128)(2,1)}, bf16[16,8,128]{2,1,0:T(8,128)(2,1)S(1)}, u32[]{:S(2)}, u32[]{:S(2)}) collective-permute-start(bf16[16,8,128]{2,1,0:T(8,128)(2,1)} %refs_0_.1), channel_id=1, source_target_pairs={{0,3},{1,2},{2,1},{3,0},{4,7},{5,6},{6,5},{7,4},{8,11},{9,10},{10,... | collective-permute-start | bytes 98312 | tf_op jit(solution)/shard_map/ppermute | solution.py:31
  7.3 4.9 %copy-start.3 = (bf16[16,8,128]{2,1,0:T(8,128)(2,1)}, bf16[16,8,128]{2,1,0:T(8,128)(2,1)S(1)}, u32[]{:S(2)}) copy-start(bf16[16,8,128]{2,1,0:T(8,128)(2,1)S(1)} %collective-permute-done.1.refs_2_) | copy-start | bytes 98308
  8.9 3.4 %copy-start.4 = (bf16[16,8,128]{2,1,0:T(8,128)(2,1)}, bf16[16,8,128]{2,1,0:T(8,128)(2,1)S(1)}, u32[]{:S(2)}) copy-start(bf16[16,8,128]{2,1,0:T(8,128)(2,1)S(1)} %collective-permute-done.refs_1_) | copy-start | bytes 98308
  12.3 0.6 %copy-start.5 = (bf16[16,8,128]{2,1,0:T(8,128)(2,1)}, bf16[16,8,128]{2,1,0:T(8,128)(2,1)S(1)}, u32[]{:S(2)}) copy-start(bf16[16,8,128]{2,1,0:T(8,128)(2,1)S(1)} %collective-permute-done.2.refs_3_) | copy-start | bytes 98308
  14.4 7.3 %collective-permute-start.5 = (bf16[32,16,128]{2,1,0:T(8,128)(2,1)}, bf16[32,16,128]{2,1,0:T(8,128)(2,1)S(1)}, u32[]{:S(2)}, u32[]{:S(2)}) collective-permute-start(bf16[32,16,128]{2,1,0:T(8,128)(2,1)} %assemble.1), channel_id=1, source_target_pairs={{0,24},{4,28},{8,16},{12,20},{16,8},{20,12},{24,0},{28,4},{1,25},{... | collective-permute-start | bytes 393224 | tf_op jit(solution)/shard_map/ppermute | solution.py:31
  16.9 5.8 %collective-permute-start.4 = (bf16[32,16,128]{2,1,0:T(8,128)(2,1)}, bf16[32,16,128]{2,1,0:T(8,128)(2,1)S(1)}, u32[]{:S(2)}, u32[]{:S(2)}) collective-permute-start(bf16[32,16,128]{2,1,0:T(8,128)(2,1)} %assemble.1), channel_id=1, source_target_pairs={{0,16},{4,20},{8,24},{12,28},{16,0},{20,4},{24,8},{28,12},{1,17},{... | collective-permute-start | bytes 393224 | tf_op jit(solution)/shard_map/ppermute | solution.py:31
  17.4 5.3 %collective-permute-start.3 = (bf16[32,16,128]{2,1,0:T(8,128)(2,1)}, bf16[32,16,128]{2,1,0:T(8,128)(2,1)S(1)}, u32[]{:S(2)}, u32[]{:S(2)}) collective-permute-start(bf16[32,16,128]{2,1,0:T(8,128)(2,1)} %assemble.1), channel_id=1, source_target_pairs={{0,8},{4,12},{8,0},{12,4},{16,24},{20,28},{24,16},{28,20},{1,9},{5... | collective-permute-start | bytes 393224 | tf_op jit(solution)/shard_map/ppermute | solution.py:31
  17.9 5.3 %collective-permute-start.6 = (bf16[32,16,128]{2,1,0:T(8,128)(2,1)}, bf16[32,16,128]{2,1,0:T(8,128)(2,1)S(1)}, u32[]{:S(2)}, u32[]{:S(2)}) collective-permute-start(bf16[32,16,128]{2,1,0:T(8,128)(2,1)} %assemble.1), channel_id=1, source_target_pairs={{0,4},{4,0},{8,12},{12,8},{16,20},{20,16},{24,28},{28,24},{1,5},{5... | collective-permute-start | bytes 393224 | tf_op jit(solution)/shard_map/ppermute | solution.py:31
  21.7 1.5 %collective-permute-start.9 = (bf16[32,16,128]{2,1,0:T(8,128)(2,1)S(1)}, bf16[32,16,128]{2,1,0:T(8,128)(2,1)S(1)}, u32[]{:S(2)}, u32[]{:S(2)}) collective-permute-start(bf16[32,16,128]{2,1,0:T(8,128)(2,1)S(1)} %collective-permute-done.5), channel_id=1, source_target_pairs={{0,4},{4,0},{8,12},{12,8},{16,20},{20,16},{24,28},{28,24},{1,5},{5... | collective-permute-start | bytes 393224 | tf_op jit(solution)/shard_map/ppermute | solution.py:31
  22.7 1.3 %collective-permute-start.8 = (bf16[32,16,128]{2,1,0:T(8,128)(2,1)S(1)}, bf16[32,16,128]{2,1,0:T(8,128)(2,1)S(1)}, u32[]{:S(2)}, u32[]{:S(2)}) collective-permute-start(bf16[32,16,128]{2,1,0:T(8,128)(2,1)S(1)} %collective-permute-done.4), channel_id=1, source_target_pairs={{0,4},{4,0},{8,12},{12,8},{16,20},{20,16},{24,28},{28,24},{1,5},{5... | collective-permute-start | bytes 393224 | tf_op jit(solution)/shard_map/ppermute | solution.py:31
  22.7 1.5 %collective-permute-start.7 = (bf16[32,16,128]{2,1,0:T(8,128)(2,1)S(1)}, bf16[32,16,128]{2,1,0:T(8,128)(2,1)S(1)}, u32[]{:S(2)}, u32[]{:S(2)}) collective-permute-start(bf16[32,16,128]{2,1,0:T(8,128)(2,1)S(1)} %collective-permute-done.3), channel_id=1, source_target_pairs={{0,4},{4,0},{8,12},{12,8},{16,20},{20,16},{24,28},{28,24},{1,5},{5... | collective-permute-start | bytes 393224 | tf_op jit(solution)/shard_map/ppermute | solution.py:31
  24.2 0.9 %copy-start = (bf16[32,16,128]{2,1,0:T(8,128)(2,1)S(1)}, bf16[32,16,128]{2,1,0:T(8,128)(2,1)}, u32[]{:S(2)}) copy-start(bf16[32,16,128]{2,1,0:T(8,128)(2,1)} %assemble.1) | copy-start | bytes 393220

commit v2 on v1

v2 whole, which is shorter than its diff:
```python
import functools
import math

import jax
import jax.numpy as jnp
import numpy as np
from jax import lax
from jax.experimental import pallas as pl
from jax.experimental.pallas import tpu as pltpu
from jax.sharding import PartitionSpec as P

epsilon = 1e-06
concentration = 40.0


def split(array):
    high = array.astype(jnp.bfloat16)
    return high, (array - high.astype(jnp.float32)).astype(jnp.bfloat16)


def angle_tables(angular):
    half = angular // 2
    product = np.outer(np.arange(half), np.arange(angular)) % angular
    phase = product.astype(np.float32) * np.float32(2.0 * math.pi / angular)
    real, imag = np.cos(phase), -np.sin(phase)
    forward = np.concatenate([real, real, imag, -imag], axis=0).astype(np.float32)
    high = forward.astype(jnp.bfloat16)
    low = (forward - high.astype(np.float32)).astype(jnp.bfloat16)
    return (
        np.concatenate([high, low], axis=1),
        np.ascontiguousarray(np.concatenate([high.T, high.T], axis=0)),
        np.ascontiguousarray(low.T),
    )


def is_power_of_two(n):
    return n & (n - 1) == 0


def moved(array, axis, pairs):
    return lax.ppermute(array, axis, pairs)


def flipped(array, axis, by):
    return moved(array, axis, [(i, i ^ by) for i in range(lax.axis_size(axis))])


def shifted(array, axis, by):
    count = lax.axis_size(axis)
    return moved(array, axis, [(i, (i + by) % count) for i in range(count)])


def slice_owner(position, step, count):
    if is_power_of_two(count):
        return position ^ step
    return (position + step) % count


def vmem():
    return pl.BlockSpec(memory_space=pltpu.VMEM)


def small_kernel(kernel, outs, count, name, limit, scratch=(), cycles=1000):
    return pl.pallas_call(
        kernel,
        out_shape=outs,
        in_specs=[vmem()] * count,
        out_specs=jax.tree.map(lambda _: vmem(), outs),
        scratch_shapes=scratch,
        compiler_params=pltpu.CompilerParams(vmem_limit_bytes=limit),
        cost_estimate=pl.CostEstimate(flops=cycles * 1024, bytes_accessed=0, transcendentals=0),
        name=name,
    )


def radial_first(source, wide, out, start):
    images, depth, angular = source.shape
    wide[...] = source[...].astype(jnp.float32).reshape(images * depth, angular)
    for r in range(depth):
        out[start + r] = wide[pl.ds(r, images, stride=depth), :].astype(out.dtype)


def turn_kernel(source, out, wide):
    radial_first(source, wide, out, 0)


def assemble_kernel(*refs):
    *slices, own, out, wide = refs
    depth = own.shape[0]
    out[:depth] = own[...]
    for k, piece in enumerate(slices[::-1]):
        radial_first(piece, wide, out, (k + 1) * depth)


def own_column(local):
    images, depth, angular = local.shape
    count = lax.axis_size("off")
    wide = [pltpu.VMEM((images * depth, angular), jnp.float32)]
    slices = [
        flipped(local, "off", k) if is_power_of_two(count) else shifted(local, "off", -k)
        for k in range(count - 1, 0, -1)
    ]
    turned = jax.ShapeDtypeStruct((depth, images, angular), local.dtype)
    whole = jax.ShapeDtypeStruct((count * depth, images, angular), local.dtype)
    own = small_kernel(turn_kernel, turned, 1, "turn", 1 << 21, wide, 100)(local)
    return small_kernel(assemble_kernel, whole, count, "assemble", 1 << 21, wide, 100)(*slices, own)


def hold_kernel(array, token, out):
    out[...] = array[...]


def hold(array, token):
    return small_kernel(
        hold_kernel, jax.ShapeDtypeStruct(array.shape, array.dtype), 2, "hold", 1 << 21, (), 100
    )(array, token)


def filter_window(column, run):
    count = lax.axis_size("blk")
    ranges = lax.axis_size("off")
    window = ranges * min(8, count // ranges)
    if window == count and count > 2 and is_power_of_two(count):
        far = [flipped(column, "blk", flip) for flip in range(count - 2, 0, -2)]
        carry = run((), [column], False)
        blocks = [hold(block, carry[2]) for block in far]
        twin = flipped(column, "blk", 1)
        carry = run(carry, blocks + [twin], False)
        return run(carry, [flipped(block, "blk", 1) for block in blocks], True)
    group = column[None]
    while group.shape[0] < window:
        held = group.shape[0]
        group = jnp.concatenate(
            [group, shifted(group[: min(held, window - held)], "blk", -held)], axis=0
        )
    return run((), [group], True)


def spread_kernel(ranges, column, direct_own, swapped_own, own_inverse, wide):
    radial, images, angular = column.shape
    rows = images // ranges
    first = lax.axis_index("off") * rows

    def step(r, squares):
        wide[r] = column[r].astype(jnp.float32)
        new = []
        for i in range(rows):
            row = wide[r, pl.ds(first + i, 1), :]
            direct_own[i, r] = jnp.broadcast_to(row, (8, angular))
            swapped_own[i, r] = jnp.broadcast_to(pltpu.roll(row, angular // 2, 1), (8, angular))
            new.append(squares[i] + row * row)
        return tuple(new)

    zero = jnp.zeros((1, angular), jnp.float32)
    squares = lax.fori_loop(0, radial, step, (zero,) * rows, unroll=8)
    for i in range(rows):
        total = jnp.sum(squares[i], axis=1, keepdims=True) + epsilon
        own_inverse[i : i + 1, :] = jnp.broadcast_to(lax.rsqrt(total), (1, angular))


def spread_own(column, ranges):
    radial, images, angular = column.shape
    rows = images // ranges
    tiles = jax.ShapeDtypeStruct((rows, radial, 8, angular), jnp.float32)
    return small_kernel(
        functools.partial(spread_kernel, ranges),
        (tiles, tiles, jax.ShapeDtypeStruct((rows, angular), jnp.float32)),
        1,
        "spread",
        1 << 22,
        [pltpu.VMEM((radial, images, angular), jnp.float32)],
        1000,
    )(column)


def fold(tiles):
    rows = tiles[0].shape[0]
    number = lax.broadcasted_iota(jnp.int32, tiles[0].shape, 0)
    step = 1
    while step < rows:
        low = (number // step) % 2 == 0
        tiles = [
            jnp.where(low, a, b) + pltpu.roll(jnp.where(low, b, a), step, 0)
            for a, b in zip(tiles[::2], tiles[1::2])
        ]
        step *= 2
    return tiles[0]


def filter_kernel(ranges, count, is_first, is_last, *refs):
    forward, backward, backward_low, direct_own, swapped_own, own_inverse, *refs = refs
    groups, refs = refs[:count], refs[count:]
    if not is_first:
        real_before, imag_before, degree_before, *refs = refs
    if is_last:
        out, log_degree, real_sum, imag_sum, *refs = refs
    else:
        real_sum, imag_sum, degrees, *refs = refs
    terms, norms, real_w, imag_w = refs
    _, radial, images, angular = groups[0].shape
    half = angular // 2
    rows = images // ranges
    depth = radial // ranges
    place = lax.axis_index("off")
    f32 = jnp.float32
    partners = images * sum(g.shape[0] for g in groups)

    def each_block(do, carry):
        start = 0
        for group in groups:
            blocks = group.shape[0]
            if blocks == 1:
                carry = do(group, 0, start, carry)
            else:

                def one(b, c, group=group, start=start):
                    return do(group, b, pl.multiple_of(start + b * images, images), c)

                carry = lax.fori_loop(0, blocks, one, carry)
            start += blocks * images
        return carry

    def cross(group, b, start, carry):
        def step(r, sums):
            direct, mixed, square = sums
            x = group[b, r].astype(f32).reshape(images // 8, 8, angular)
            direct = tuple(direct[i] + direct_own[i, r][None] * x for i in range(rows))
            mixed = tuple(mixed[i] + swapped_own[i, r][None] * x for i in range(rows))
            return direct, mixed, square + x * x

        zero = jnp.zeros((images // 8, 8, angular), f32)
        direct, mixed, square = lax.fori_loop(
            0, radial, step, ((zero,) * rows, (zero,) * rows, zero), unroll=True
        )
        for i in range(rows):
            at = pl.ds(i * partners + start, images)
            terms[at, :angular] = direct[i].reshape(images, angular)
            terms[at, angular:] = mixed[i].reshape(images, angular)
        norms[pl.ds(start, images), :] = square.reshape(images, angular)
        return carry

    each_block(cross, 0)

    high, low = split(terms[...])
    both = jnp.dot(high, forward[...], preferred_element_type=f32)
    rest = jnp.dot(low, forward[:, :angular], preferred_element_type=f32)
    correlation = both[:, :angular] + (both[:, angular:] + rest)
    inverse = lax.rsqrt(jnp.sum(norms[...], axis=1, keepdims=True) + epsilon) * concentration
    weights = []
    for i in range(rows):
        exponent = correlation[i * partners : (i + 1) * partners] * own_inverse[i : i + 1] * inverse
        weight = jnp.exp(exponent)
        if is_first:
            numbers = lax.broadcasted_iota(jnp.int32, (partners, angular), 0)
            weight = jnp.where(numbers == place * rows + i, 0.0, weight)
        weights.append(weight)
    high, low = split(jnp.concatenate(weights, axis=0))
    spectral = jnp.dot(jnp.concatenate([high, low], axis=1), backward[...], preferred_element_type=f32)
    spectral = spectral + jnp.dot(high, backward_low[...], preferred_element_type=f32)
    scales = []
    for i in range(rows):
        part = spectral[i * partners : (i + 1) * partners]
        degree = jnp.sum(part[:, :angular], axis=0, keepdims=True)
        if not is_first:
            degree = degree + degree_before[i : i + 1]
        if is_last:
            scales.append(1.0 / degree[:, :1])
            log_degree[i] = jnp.log(degree)[0, 0]
        else:
            degrees[i : i + 1, :] = degree
        real_w[i] = part[:, :angular].astype(jnp.bfloat16).astype(f32)
        imag_w[i] = part[:, angular:].astype(jnp.bfloat16).astype(f32)

    def filtered(pair, carry):
        places = (2 * pair, 2 * pair + 1)
        if is_first:
            zero = jnp.zeros((8, angular), f32)
            start_sums = (((zero,) * rows, (zero,) * rows),) * 2
        else:
            start_sums = tuple(
                (
                    tuple(real_before[i, r] for i in range(rows)),
                    tuple(imag_before[i, r] for i in range(rows)),
                )
                for r in places
            )

        def accumulate(group, b, start, sums):
            new = [(list(s[0]), list(s[1])) for s in sums]
            xs = [group[b, r].astype(f32) for r in places]
            for v in range(images // 8):
                for i in range(rows):
                    real = real_w[i, pl.ds(start + 8 * v, 8), :]
                    imag = imag_w[i, pl.ds(start + 8 * v, 8), :]
                    for n in range(2):
                        x = xs[n][8 * v : 8 * v + 8]
                        new[n][0][i] = new[n][0][i] + real * x
                        new[n][1][i] = new[n][1][i] + imag * x
            return tuple((tuple(a), tuple(b)) for a, b in new)

        totals = each_block(accumulate, start_sums)
        for n in range(2):
            for i in range(rows):
                real_sum[i, places[n]] = totals[n][0][i]
                imag_sum[i, places[n]] = totals[n][1][i]
        return carry

    lax.fori_loop(0, radial // 2, filtered, 0, unroll=2)

    if is_last:
        for k in range(ranges):
            for part in range(depth // 8):
                at = k * depth + 8 * part
                target = slice_owner(place, k, ranges) * depth + 8 * part
                for i in range(rows):
                    real = fold([real_sum[i, at + n] for n in range(8)])
                    imag = fold([imag_sum[i, at + n] for n in range(8)])
                    total = real + pltpu.roll(imag, half, 1)
                    out[i, pl.ds(pl.multiple_of(target, 8), 8), :] = total * scales[i]


def filter_stage(ranges, own, tables, carry, groups, is_last):
    groups = [g.reshape(-1, *g.shape[-3:]) for g in groups]
    _, radial, images, angular = groups[0].shape
    rows = images // ranges
    f32 = jnp.float32
    sums = jax.ShapeDtypeStruct((rows, radial, 8, angular), f32)
    partners = images * sum(g.shape[0] for g in groups)
    scratch = [
        pltpu.VMEM((rows * partners, 2 * angular), f32),
        pltpu.VMEM((partners, angular), f32),
        pltpu.VMEM((rows, partners, angular), f32),
        pltpu.VMEM((rows, partners, angular), f32),
    ]
    if is_last:
        outs = (
            jax.ShapeDtypeStruct((rows, radial, angular), f32),
            jax.ShapeDtypeStruct((rows,), f32),
        )
        out_specs = (vmem(), pl.BlockSpec(memory_space=pltpu.SMEM))
        scratch = [pltpu.VMEM(sums.shape, f32)] * 2 + scratch
    else:
        outs = (sums, sums, jax.ShapeDtypeStruct((rows, angular), f32))
        out_specs = (vmem(),) * 3
    operands = (*tables, *own, *groups, *carry)
    return pl.pallas_call(
        functools.partial(filter_kernel, ranges, len(groups), not carry, is_last),
        out_shape=outs,
        in_specs=[vmem()] * len(operands),
        out_specs=out_specs,
        scratch_shapes=scratch,
        compiler_params=pltpu.CompilerParams(
            vmem_limit_bytes=(40 if partners > 8 * images else 8) << 20
        ),
        cost_estimate=pl.CostEstimate(
            flops=4 * partners * radial * 1024 * rows, bytes_accessed=0, transcendentals=0
        ),
        name="filter",
    )(*operands)


def body(coefficients):
    ranges = lax.axis_size("off")
    column = own_column(coefficients)
    own = spread_own(column, ranges)
    tables = angle_tables(coefficients.shape[2])
    return filter_window(column, functools.partial(filter_stage, ranges, own, tables))


def solution(mesh):
    return jax.shard_map(
        body,
        mesh=mesh,
        in_specs=(P("blk", "off", None),),
        out_specs=(P(("blk", "off"), None, None), P(("blk", "off"))),
        check_vma=False,
    )
```

time: 34.7 us -> 23.4 us (0.67)
  Pallas kernels: 10.3 us -> 4.96 us
  waiting for transfers between devices: 11.7 us -> 6.79 us
  local copies, waits for them, and re-layouts: 2.17 us -> 0.81 us
    pallas_call x2 -> x9, Pallas kernels: 10.3 us -> 4.96 us  [the longest x3 4.31 us: filter_stage(): pl.pallas_call(functools.partial(filter_kernel, ranges, len(groups), not...]
    ppermute x10, waiting for transfers between devices: 11.7 us -> 6.79 us  [moved(): return lax.ppermute(array, axis, pairs)]
    unnamed x12 -> x8, local copies, waits for them, and re-layouts: 1.55 us -> 0.81 us
    slice x1 -> x0, local copies, waits for them, and re-layouts: 0.63 us -> none  [body(): return (smoothed, log_degree[:, 0])]
  transfers between devices with their start and end apart: 10 -> 10, of which waited for: 7 -> 4; matrix products, arithmetic and copies ran while one was open for 0% -> 0% of each run, Pallas kernels for 0% -> 12%
where the time goes in v2:
time: 23.4 us; the launch traced here: 23.2 us
  starting transfers between devices  9.93 us (42%)
  waiting for transfers between devices  6.79 us (29%)
  Pallas kernels  4.96 us (21%)
  local copies, waits for them, and re-layouts  0.81 us (3%)
  between operations  0.76 us (3%)
    ppermute x10, starting transfers between devices, moved(): return lax.ppermute(array, axis, pairs)  9.93 us
    ppermute x10, waiting for transfers between devices, moved(): return lax.ppermute(array, axis, pairs)  6.79 us
    pallas_call x3, Pallas kernels, filter_stage(): pl.pallas_call(functools.partial(filter_kernel, ranges, len(groups), not...  4.31 us
    unnamed x8, local copies, waits for them, and re-layouts  0.81 us
    pallas_call x1, Pallas kernels, spread_own(): small_kernel(functools.partial(spread_kernel, ranges), (tiles, tiles, jax...  0.55 us
  transfers between devices with their start and end apart: 10, of which 4 were waited for; matrix products, arithmetic and copies ran while one was open for 0% of the time, Pallas kernels for 12%

profile of v2, /device:TPU:0, one launch (start us, length us, event | category | flops | bytes accessed | tf_op | source)
XLA Modules:
  0.0 23.2 jit_solution(2343391582562978909)
XLA Ops:
  0.6 4.1 %collective-permute-start.1 = (bf16[16,8,128]{2,1,0:T(8,128)(2,1)}, bf16[16,8,128]{2,1,0:T(8,128)(2,1)S(1)}, u32[]{:S(2)}, u32[]{:S(2)}) collective-permute-start(bf16[16,8,128]{2,1,0:T(8,128)(2,1)} %source.1), channel_id=1, source_target_pairs={{0,2},{1,3},{2,0},{3,1},{4,6},{5,7},{6,4},{7,5},{8,10},{9,11},{10,... | collective-permute-start | bytes 98312 | tf_op jit(solution)/shard_map/ppermute | solution.py:41
  4.7 1.3 %collective-permute-start = (bf16[16,8,128]{2,1,0:T(8,128)(2,1)}, bf16[16,8,128]{2,1,0:T(8,128)(2,1)S(1)}, u32[]{:S(2)}, u32[]{:S(2)}) collective-permute-start(bf16[16,8,128]{2,1,0:T(8,128)(2,1)} %source.1), channel_id=1, source_target_pairs={{0,3},{1,2},{2,1},{3,0},{4,7},{5,6},{6,5},{7,4},{8,11},{9,10},{10,... | collective-permute-start | bytes 98312 | tf_op jit(solution)/shard_map/ppermute | solution.py:41
  6.1 0.2 collective-permute-start.2
  6.3 0.0 copy-start.3
  6.3 0.8 %copy-done.3 = bf16[16,8,128]{2,1,0:T(8,128)(2,1)S(1)} copy-done((bf16[16,8,128]{2,1,0:T(8,128)(2,1)S(1)}, bf16[16,8,128]{2,1,0:T(8,128)(2,1)}, u32[]{:S(2)}) %copy-start.3) | copy-done | bytes 32792
  7.1 0.1 collective-permute-done.1.refs_1_
  7.2 3.5 %collective-permute-done.refs_0_ = bf16[16,8,128]{2,1,0:T(8,128)(2,1)S(1)} collective-permute-done((bf16[16,8,128]{2,1,0:T(8,128)(2,1)}, bf16[16,8,128]{2,1,0:T(8,128)(2,1)S(1)}, u32[]{:S(2)}, u32[]{:S(2)}) %collective-permute-start) | collective-permute-done | bytes 32800 | tf_op jit(solution)/shard_map/ppermute | solution.py:41
  10.7 0.0 collective-permute-done.2.refs_2_
  10.7 0.0 copy-start.1
  10.7 0.0 copy-start.2
  10.7 0.1 assemble.1.column
  10.7 0.0 copy-start
  10.7 2.5 %collective-permute-start.3 = (bf16[32,16,128]{2,1,0:T(8,128)(2,1)S(1)}, bf16[32,16,128]{2,1,0:T(8,128)(2,1)S(1)}, u32[]{:S(2)}, u32[]{:S(2)}) collective-permute-start(bf16[32,16,128]{2,1,0:T(8,128)(2,1)S(1)} %assemble.1.column), channel_id=1, source_target_pairs={{0,24},{4,28},{8,16},{12,20},{16,8},{20,12},{24,0},{28,4},{1,25},{... | collective-permute-start | bytes 393224 | tf_op jit(solution)/shard_map/ppermute | solution.py:41
  13.2 0.5 %collective-permute-start.5 = (bf16[32,16,128]{2,1,0:T(8,128)(2,1)S(1)}, bf16[32,16,128]{2,1,0:T(8,128)(2,1)S(1)}, u32[]{:S(2)}, u32[]{:S(2)}) collective-permute-start(bf16[32,16,128]{2,1,0:T(8,128)(2,1)S(1)} %assemble.1.column), channel_id=1, source_target_pairs={{0,16},{4,20},{8,24},{12,28},{16,0},{20,4},{24,8},{28,12},{1,17},{... | collective-permute-start | bytes 393224 | tf_op jit(solution)/shard_map/ppermute | solution.py:41
  13.8 0.5 %collective-permute-start.7 = (bf16[32,16,128]{2,1,0:T(8,128)(2,1)S(1)}, bf16[32,16,128]{2,1,0:T(8,128)(2,1)S(1)}, u32[]{:S(2)}, u32[]{:S(2)}) collective-permute-start(bf16[32,16,128]{2,1,0:T(8,128)(2,1)S(1)} %assemble.1.column), channel_id=1, source_target_pairs={{0,8},{4,12},{8,0},{12,4},{16,24},{20,28},{24,16},{28,20},{1,9},{5... | collective-permute-start | bytes 393224 | tf_op jit(solution)/shard_map/ppermute | solution.py:41
  14.3 0.0 collective-permute-start.9
  14.3 0.6 %spread.1 = (f32[4,32,8,128]{3,2,1,0:T(8,128)S(1)}, f32[4,32,8,128]{3,2,1,0:T(8,128)S(1)}, f32[4,128]{1,0:T(4,128)S(1)}) custom-call(bf16[32,16,128]{2,1,0:T(8,128)(2,1)S(1)} %assemble.1.column), custom_call_target="tpu_custom_call" | custom-call | flops 1024000 | tf_op jit(solution)/shard_map/spread/pallas_call | solution.py:165
  14.8 0.0 copy-done.1
  14.8 0.0 copy-done.2
  14.9 0.0 copy-done
  14.9 0.6 %filter.3 = (f32[4,32,8,128]{3,2,1,0:T(8,128)S(1)}, f32[4,32,8,128]{3,2,1,0:T(8,128)S(1)}, f32[4,128]{1,0:T(4,128)S(1)}) custom-call(bf16[256,256]{1,0:T(8,128)(2,1)S(1)} %copy-done.1, bf16[256,256]{1,0:T(8,128)(2,1)S(1)} %copy-done, bf16[128,256]{1,0:T(8,128)(2,1)S(1)} %copy-done.2, f32[4,32,8,128]{3,2,1,0:T(8,128)S(1)} %get-tuple-element.11.refs_3_, ...), custom_call_target="tpu_custom_call" | custom-call | flops 8388608 | tf_op jit(solution)/shard_map/filter/pallas_call | solution.py:346
  15.5 2.6 %collective-permute-done.3.array = bf16[32,16,128]{2,1,0:T(8,128)(2,1)S(1)} collective-permute-done((bf16[32,16,128]{2,1,0:T(8,128)(2,1)S(1)}, bf16[32,16,128]{2,1,0:T(8,128)(2,1)S(1)}, u32[]{:S(2)}, u32[]{:S(2)}) %collective-permute-start.3) | collective-permute-done | bytes 131104 | tf_op jit(solution)/shard_map/ppermute | solution.py:41
  18.1 0.1 collective-permute-start.4
  18.2 0.7 %collective-permute-done.5.array = bf16[32,16,128]{2,1,0:T(8,128)(2,1)S(1)} collective-permute-done((bf16[32,16,128]{2,1,0:T(8,128)(2,1)S(1)}, bf16[32,16,128]{2,1,0:T(8,128)(2,1)S(1)}, u32[]{:S(2)}, u32[]{:S(2)}) %collective-permute-start.5) | collective-permute-done | bytes 131104 | tf_op jit(solution)/shard_map/ppermute | solution.py:41
  18.9 0.1 collective-permute-start.6
  18.9 0.0 collective-permute-done.7.array
  19.0 0.5 %collective-permute-start.8 = (bf16[32,16,128]{2,1,0:T(8,128)(2,1)S(1)}, bf16[32,16,128]{2,1,0:T(8,128)(2,1)S(1)}, u32[]{:S(2)}, u32[]{:S(2)}) collective-permute-start(bf16[32,16,128]{2,1,0:T(8,128)(2,1)S(1)} %hold.5), channel_id=1, source_target_pairs={{0,4},{4,0},{8,12},{12,8},{16,20},{20,16},{24,28},{28,24},{1,5},{5... | collective-permute-start | bytes 393224 | tf_op jit(solution)/shard_map/ppermute | solution.py:41
  19.5 0.0 collective-permute-done.9
  19.5 1.6 %filter.4 = (f32[4,32,8,128]{3,2,1,0:T(8,128)S(1)}, f32[4,32,8,128]{3,2,1,0:T(8,128)S(1)}, f32[4,128]{1,0:T(4,128)S(1)}) custom-call(bf16[256,256]{1,0:T(8,128)(2,1)S(1)} %copy-done.1, bf16[256,256]{1,0:T(8,128)(2,1)S(1)} %copy-done, bf16[128,256]{1,0:T(8,128)(2,1)S(1)} %copy-done.2, f32[4,32,8,128]{3,2,1,0:T(8,128)S(1)} %get-tuple-element.11.refs_3_, ...), custom_call_target="tpu_custom_call" | custom-call | flops 33554432 | tf_op jit(solution)/shard_map/filter/pallas_call | solution.py:346
  21.1 0.0 collective-permute-done.4
  21.1 0.0 collective-permute-done.6
  21.1 0.0 collective-permute-done.8
  21.2 2.1 %filter.5 = (f32[4,32,128]{2,1,0:T(8,128)}, f32[4]{0:T(128)}) custom-call(bf16[256,256]{1,0:T(8,128)(2,1)S(1)} %copy-done.1, bf16[256,256]{1,0:T(8,128)(2,1)S(1)} %copy-done, bf16[128,256]{1,0:T(8,128)(2,1)S(1)} %copy-done.2, f32[4,32,8,128]{3,2,1,0:T(8,128)S(1)} %get-tuple-element.11.refs_3_, f32[4,32,8,128]{3,2,1,0:T(8,128)S(1)} %get-tuple-element.12.refs_4_, ...), custom_call_target="tpu_custom_call" | custom-call | flops 25165824 | tf_op jit(solution)/shard_map/filter/pallas_call | solution.py:346
  (4 shorter events, 0.1 us)
Async XLA Ops:
  0.6 6.6 %collective-permute-start.1 = (bf16[16,8,128]{2,1,0:T(8,128)(2,1)}, bf16[16,8,128]{2,1,0:T(8,128)(2,1)S(1)}, u32[]{:S(2)}, u32[]{:S(2)}) collective-permute-start(bf16[16,8,128]{2,1,0:T(8,128)(2,1)} %source.1), channel_id=1, source_target_pairs={{0,2},{1,3},{2,0},{3,1},{4,6},{5,7},{6,4},{7,5},{8,10},{9,11},{10,... | collective-permute-start | bytes 98312 | tf_op jit(solution)/shard_map/ppermute | solution.py:41
  4.7 5.9 %collective-permute-start = (bf16[16,8,128]{2,1,0:T(8,128)(2,1)}, bf16[16,8,128]{2,1,0:T(8,128)(2,1)S(1)}, u32[]{:S(2)}, u32[]{:S(2)}) collective-permute-start(bf16[16,8,128]{2,1,0:T(8,128)(2,1)} %source.1), channel_id=1, source_target_pairs={{0,3},{1,2},{2,1},{3,0},{4,7},{5,6},{6,5},{7,4},{8,11},{9,10},{10,... | collective-permute-start | bytes 98312 | tf_op jit(solution)/shard_map/ppermute | solution.py:41
  6.1 4.6 %collective-permute-start.2 = (bf16[16,8,128]{2,1,0:T(8,128)(2,1)}, bf16[16,8,128]{2,1,0:T(8,128)(2,1)S(1)}, u32[]{:S(2)}, u32[]{:S(2)}) collective-permute-start(bf16[16,8,128]{2,1,0:T(8,128)(2,1)} %source.1), channel_id=1, source_target_pairs={{0,1},{1,0},{2,3},{3,2},{4,5},{5,4},{6,7},{7,6},{8,9},{9,8},{10,11... | collective-permute-start | bytes 98312 | tf_op jit(solution)/shard_map/ppermute | solution.py:41
  6.3 0.8 %copy-start.3 = (bf16[16,8,128]{2,1,0:T(8,128)(2,1)S(1)}, bf16[16,8,128]{2,1,0:T(8,128)(2,1)}, u32[]{:S(2)}) copy-start(bf16[16,8,128]{2,1,0:T(8,128)(2,1)} %source.1) | copy-start | bytes 98308
  10.7 4.2 %copy-start.1 = (bf16[256,256]{1,0:T(8,128)(2,1)S(1)}, bf16[256,256]{1,0:T(8,128)(2,1)}, u32[]{:S(2)}) copy-start(bf16[256,256]{1,0:T(8,128)(2,1)} %constant.6.clone.refs_0_) | copy-start | bytes 393220
  10.7 4.2 %copy-start.2 = (bf16[128,256]{1,0:T(8,128)(2,1)S(1)}, bf16[128,256]{1,0:T(8,128)(2,1)}, u32[]{:S(2)}) copy-start(bf16[128,256]{1,0:T(8,128)(2,1)} %constant.8.clone.refs_2_) | copy-start | bytes 196612
  10.7 4.1 %copy-start = (bf16[256,256]{1,0:T(8,128)(2,1)S(1)}, bf16[256,256]{1,0:T(8,128)(2,1)}, u32[]{:S(2)}) copy-start(bf16[256,256]{1,0:T(8,128)(2,1)} %constant.7.clone.refs_1_) | copy-start | bytes 393220
  10.7 7.3 %collective-permute-start.3 = (bf16[32,16,128]{2,1,0:T(8,128)(2,1)S(1)}, bf16[32,16,128]{2,1,0:T(8,128)(2,1)S(1)}, u32[]{:S(2)}, u32[]{:S(2)}) collective-permute-start(bf16[32,16,128]{2,1,0:T(8,128)(2,1)S(1)} %assemble.1.column), channel_id=1, source_target_pairs={{0,24},{4,28},{8,16},{12,20},{16,8},{20,12},{24,0},{28,4},{1,25},{... | collective-permute-start | bytes 393224 | tf_op jit(solution)/shard_map/ppermute | solution.py:41
  13.2 5.6 %collective-permute-start.5 = (bf16[32,16,128]{2,1,0:T(8,128)(2,1)S(1)}, bf16[32,16,128]{2,1,0:T(8,128)(2,1)S(1)}, u32[]{:S(2)}, u32[]{:S(2)}) collective-permute-start(bf16[32,16,128]{2,1,0:T(8,128)(2,1)S(1)} %assemble.1.column), channel_id=1, source_target_pairs={{0,16},{4,20},{8,24},{12,28},{16,0},{20,4},{24,8},{28,12},{1,17},{... | collective-permute-start | bytes 393224 | tf_op jit(solution)/shard_map/ppermute | solution.py:41
  13.8 5.2 %collective-permute-start.7 = (bf16[32,16,128]{2,1,0:T(8,128)(2,1)S(1)}, bf16[32,16,128]{2,1,0:T(8,128)(2,1)S(1)}, u32[]{:S(2)}, u32[]{:S(2)}) collective-permute-start(bf16[32,16,128]{2,1,0:T(8,128)(2,1)S(1)} %assemble.1.column), channel_id=1, source_target_pairs={{0,8},{4,12},{8,0},{12,4},{16,24},{20,28},{24,16},{28,20},{1,9},{5... | collective-permute-start | bytes 393224 | tf_op jit(solution)/shard_map/ppermute | solution.py:41
  14.3 5.2 %collective-permute-start.9 = (bf16[32,16,128]{2,1,0:T(8,128)(2,1)S(1)}, bf16[32,16,128]{2,1,0:T(8,128)(2,1)S(1)}, u32[]{:S(2)}, u32[]{:S(2)}) collective-permute-start(bf16[32,16,128]{2,1,0:T(8,128)(2,1)S(1)} %assemble.1.column), channel_id=1, source_target_pairs={{0,4},{4,0},{8,12},{12,8},{16,20},{20,16},{24,28},{28,24},{1,5},{5... | collective-permute-start | bytes 393224 | tf_op jit(solution)/shard_map/ppermute | solution.py:41
  18.1 3.0 %collective-permute-start.4 = (bf16[32,16,128]{2,1,0:T(8,128)(2,1)S(1)}, bf16[32,16,128]{2,1,0:T(8,128)(2,1)S(1)}, u32[]{:S(2)}, u32[]{:S(2)}) collective-permute-start(bf16[32,16,128]{2,1,0:T(8,128)(2,1)S(1)} %hold.3), channel_id=1, source_target_pairs={{0,4},{4,0},{8,12},{12,8},{16,20},{20,16},{24,28},{28,24},{1,5},{5... | collective-permute-start | bytes 393224 | tf_op jit(solution)/shard_map/ppermute | solution.py:41
  18.9 2.3 %collective-permute-start.6 = (bf16[32,16,128]{2,1,0:T(8,128)(2,1)S(1)}, bf16[32,16,128]{2,1,0:T(8,128)(2,1)S(1)}, u32[]{:S(2)}, u32[]{:S(2)}) collective-permute-start(bf16[32,16,128]{2,1,0:T(8,128)(2,1)S(1)} %hold.4), channel_id=1, source_target_pairs={{0,4},{4,0},{8,12},{12,8},{16,20},{20,16},{24,28},{28,24},{1,5},{5... | collective-permute-start | bytes 393224 | tf_op jit(solution)/shard_map/ppermute | solution.py:41
  19.0 2.2 %collective-permute-start.8 = (bf16[32,16,128]{2,1,0:T(8,128)(2,1)S(1)}, bf16[32,16,128]{2,1,0:T(8,128)(2,1)S(1)}, u32[]{:S(2)}, u32[]{:S(2)}) collective-permute-start(bf16[32,16,128]{2,1,0:T(8,128)(2,1)S(1)} %hold.5), channel_id=1, source_target_pairs={{0,4},{4,0},{8,12},{12,8},{16,20},{20,16},{24,28},{28,24},{1,5},{5... | collective-permute-start | bytes 393224 | tf_op jit(solution)/shard_map/ppermute | solution.py:41

commit v3 on v2

--- a/solution.py
+++ b/solution.py
@@ -50,12 +50,6 @@
     return moved(array, axis, [(i, (i + by) % count) for i in range(count)])
 
 
-def slice_owner(position, step, count):
-    if is_power_of_two(count):
-        return position ^ step
-    return (position + step) % count
-
-
 def vmem():
     return pl.BlockSpec(memory_space=pltpu.VMEM)
 
@@ -78,62 +72,6 @@
     wide[...] = source[...].astype(jnp.float32).reshape(images * depth, angular)
     for r in range(depth):
         out[start + r] = wide[pl.ds(r, images, stride=depth), :].astype(out.dtype)
-
-
-def turn_kernel(source, out, wide):
-    radial_first(source, wide, out, 0)
-
-
-def assemble_kernel(*refs):
-    *slices, own, out, wide = refs
-    depth = own.shape[0]
-    out[:depth] = own[...]
-    for k, piece in enumerate(slices[::-1]):
-        radial_first(piece, wide, out, (k + 1) * depth)
-
-
-def own_column(local):
-    images, depth, angular = local.shape
-    count = lax.axis_size("off")
-    wide = [pltpu.VMEM((images * depth, angular), jnp.float32)]
-    slices = [
-        flipped(local, "off", k) if is_power_of_two(count) else shifted(local, "off", -k)
-        for k in range(count - 1, 0, -1)
-    ]
-    turned = jax.ShapeDtypeStruct((depth, images, angular), local.dtype)
-    whole = jax.ShapeDtypeStruct((count * depth, images, angular), local.dtype)
-    own = small_kernel(turn_kernel, turned, 1, "turn", 1 << 21, wide, 100)(local)
-    return small_kernel(assemble_kernel, whole, count, "assemble", 1 << 21, wide, 100)(*slices, own)
-
-
-def hold_kernel(array, token, out):
-    out[...] = array[...]
-
-
-def hold(array, token):
-    return small_kernel(
-        hold_kernel, jax.ShapeDtypeStruct(array.shape, array.dtype), 2, "hold", 1 << 21, (), 100
-    )(array, token)
-
-
-def filter_window(column, run):
-    count = lax.axis_size("blk")
-    ranges = lax.axis_size("off")
-    window = ranges * min(8, count // ranges)
-    if window == count and count > 2 and is_power_of_two(count):
-        far = [flipped(column, "blk", flip) for flip in range(count - 2, 0, -2)]
-        carry = run((), [column], False)
-        blocks = [hold(block, carry[2]) for block in far]
-        twin = flipped(column, "blk", 1)
-        carry = run(carry, blocks + [twin], False)
-        return run(carry, [flipped(block, "blk", 1) for block in blocks], True)
-    group = column[None]
-    while group.shape[0] < window:
-        held = group.shape[0]
-        group = jnp.concatenate(
-            [group, shifted(group[: min(held, window - held)], "blk", -held)], axis=0
-        )
-    return run((), [group], True)
 
 
 def spread_kernel(ranges, column, direct_own, swapped_own, own_inverse, wide):
@@ -187,7 +125,7 @@
     return tiles[0]
 
 
-def filter_kernel(ranges, count, is_first, is_last, *refs):
+def filter_kernel(ranges, slice_place, count, is_first, is_last, *refs):
     forward, backward, backward_low, direct_own, swapped_own, own_inverse, *refs = refs
     groups, refs = refs[:count], refs[count:]
     if not is_first:
@@ -311,7 +249,7 @@
         for k in range(ranges):
             for part in range(depth // 8):
                 at = k * depth + 8 * part
-                target = slice_owner(place, k, ranges) * depth + 8 * part
+                target = slice_place(place, k) * depth + 8 * part
                 for i in range(rows):
                     real = fold([real_sum[i, at + n] for n in range(8)])
                     imag = fold([imag_sum[i, at + n] for n in range(8)])
@@ -319,7 +257,8 @@
                     out[i, pl.ds(pl.multiple_of(target, 8), 8), :] = total * scales[i]
 
 
-def filter_stage(ranges, own, tables, carry, groups, is_last):
+def filter_stage(tables, slice_place, own, carry, groups, is_last):
+    ranges = lax.axis_size("off")
     groups = [g.reshape(-1, *g.shape[-3:]) for g in groups]
     _, radial, images, angular = groups[0].shape
     rows = images // ranges
@@ -344,7 +283,7 @@
         out_specs = (vmem(),) * 3
     operands = (*tables, *own, *groups, *carry)
     return pl.pallas_call(
-        functools.partial(filter_kernel, ranges, len(groups), not carry, is_last),
+        functools.partial(filter_kernel, ranges, slice_place, len(groups), not carry, is_last),
         out_shape=outs,
         in_specs=[vmem()] * len(operands),
         out_specs=out_specs,
@@ -359,12 +298,72 @@
     )(*operands)
 
 
+def assemble_kernel(*refs):
+    *slices, out, wide = refs
+    depth = slices[0].shape[1]
+    for k, piece in enumerate(slices[::-1]):
+        radial_first(piece, wide, out, k * depth)
+
+
+def assemble(slices):
+    images, depth, angular = slices[0].shape
+    whole = jax.ShapeDtypeStruct((len(slices) * depth, images, angular), slices[0].dtype)
+    wide = [pltpu.VMEM((images * depth, angular), jnp.float32)]
+    return small_kernel(assemble_kernel, whole, len(slices), "assemble", 1 << 21, wide, 100)(*slices)
+
+
+def join_kernel(first, rest, token, out):
+    depth = first.shape[0]
+    out[:depth] = first[...]
+    out[depth:] = rest[...]
+
+
+def join(first, rest, token):
+    depth, images, angular = rest.shape
+    whole = jax.ShapeDtypeStruct((first.shape[0] + depth, images, angular), rest.dtype)
+    return small_kernel(join_kernel, whole, 3, "join", 1 << 21, (), 100)(first, rest, token)
+
+
+def by_flips(local, run):
+    depth = local.shape[1]
+    far = range(lax.axis_size("blk") - 2, 0, -2)
+    slices = [flipped(local, "off", k) for k in range(lax.axis_size("off") - 1, 0, -1)]
+    heads = assemble([flipped(local, "blk", flip) for flip in far][::-1] + [local])
+    head = [heads[n * depth : (n + 1) * depth] for n in range(len(far) + 1)]
+    rest = assemble(slices)
+    rests = [flipped(rest, "blk", flip) for flip in far]
+    column = join(head[0], rest, heads)
+    run = functools.partial(run, spread_own(column, lax.axis_size("off")))
+    carry = run((), [column], False)
+    first = join(head[1], rests[0], carry[2])
+    carry = run(carry, [first], False)
+    others = [join(h, r, carry[2]) for h, r in zip(head[2:], rests[1:])]
+    twins = [flipped(block, "blk", 1) for block in [column, first] + others]
+    carry = run(carry, others + twins[:2], not others)
+    return run(carry, twins[2:], True) if others else carry
+
+
+def by_shifts(local, window, run):
+    ranges = lax.axis_size("off")
+    column = assemble([shifted(local, "off", -k) for k in range(ranges - 1, 0, -1)] + [local])
+    group = column[None]
+    while group.shape[0] < window:
+        held = group.shape[0]
+        more = shifted(group[: min(held, window - held)], "blk", -held)
+        group = jnp.concatenate([group, more], axis=0)
+    return run(spread_own(column, ranges), (), [group], True)
+
+
 def body(coefficients):
-    ranges = lax.axis_size("off")
-    column = own_column(coefficients)
-    own = spread_own(column, ranges)
+    count, ranges = lax.axis_size("blk"), lax.axis_size("off")
+    window = ranges * min(8, count // ranges)
     tables = angle_tables(coefficients.shape[2])
-    return filter_window(column, functools.partial(filter_stage, ranges, own, tables))
+    flips = window == count and count > 2 and ranges > 1
+    if flips and is_power_of_two(count) and is_power_of_two(ranges):
+        stage = functools.partial(filter_stage, tables, lambda place, k: place ^ k)
+        return by_flips(coefficients, stage)
+    stage = functools.partial(filter_stage, tables, lambda place, k: (place + k) % ranges)
+    return by_shifts(coefficients, window, stage)
 
 
 def solution(mesh):

time: 23.4 us -> 22.3 us (0.953)
  waiting for transfers between devices: 6.79 us -> 1.51 us
  starting transfers between devices: 9.93 us -> 14 us
  Pallas kernels: 4.96 us -> 5.44 us
  local copies, waits for them, and re-layouts: 0.81 us -> 0.35 us
    ppermute x10 -> x13, waiting for transfers between devices: 6.79 us -> 1.51 us  [moved(): return lax.ppermute(array, axis, pairs)]
    ppermute x10 -> x13, starting transfers between devices: 9.93 us -> 14 us  [moved(): return lax.ppermute(array, axis, pairs)]
    pallas_call x8 -> x10, Pallas kernels: 4.41 us -> 4.88 us  [the longest x4 4.73 us: filter_stage(): pl.pallas_call(functools.partial(filter_kernel, ranges, slice_place, len(...]
    unnamed x8, local copies, waits for them, and re-layouts: 0.81 us -> 0.34 us
  transfers between devices with their start and end apart: 10 -> 13, of which waited for: 4 -> 4; matrix products, arithmetic and copies ran while one was open for 0% -> 0% of each run, Pallas kernels for 12% -> 16%
where the time goes in v3:
time: 22.3 us; the launch traced here: 22.1 us
  starting transfers between devices  14 us (63%)
  Pallas kernels  5.44 us (24%)
  waiting for transfers between devices  1.51 us (7%)
  between operations  0.78 us (3%)
  local copies, waits for them, and re-layouts  0.35 us (2%)
    ppermute x13, starting transfers between devices, moved(): return lax.ppermute(array, axis, pairs)  14 us
    pallas_call x4, Pallas kernels, filter_stage(): pl.pallas_call(functools.partial(filter_kernel, ranges, slice_place, len(...  4.73 us
    ppermute x13, waiting for transfers between devices, moved(): return lax.ppermute(array, axis, pairs)  1.51 us
    pallas_call x1, Pallas kernels, spread_own(): small_kernel(functools.partial(spread_kernel, ranges), (tiles, tiles, jax...  0.56 us
  transfers between devices with their start and end apart: 13, of which 4 were waited for; matrix products, arithmetic and copies ran while one was open for 0% of the time, Pallas kernels for 16%

profile of v3, /device:TPU:0, one launch (start us, length us, event | category | flops | bytes accessed | tf_op | source)
XLA Modules:
  0.0 22.1 jit_solution(2504113982422644706)
XLA Ops:
  0.6 0.0 copy-start.3
  0.6 5.1 %collective-permute-start.3 = (bf16[16,8,128]{2,1,0:T(8,128)(2,1)}, bf16[16,8,128]{2,1,0:T(8,128)(2,1)S(1)}, u32[]{:S(2)}, u32[]{:S(2)}) collective-permute-start(bf16[16,8,128]{2,1,0:T(8,128)(2,1)} %refs_3_.1), channel_id=1, source_target_pairs={{0,3},{1,2},{2,1},{3,0},{4,7},{5,6},{6,5},{7,4},{8,11},{9,10},{10,... | collective-permute-start | bytes 98312 | tf_op jit(solution)/shard_map/ppermute | solution.py:41
  5.8 0.0 collective-permute-start.4
  5.8 0.6 %collective-permute-start.5 = (bf16[16,8,128]{2,1,0:T(8,128)(2,1)}, bf16[16,8,128]{2,1,0:T(8,128)(2,1)S(1)}, u32[]{:S(2)}, u32[]{:S(2)}) collective-permute-start(bf16[16,8,128]{2,1,0:T(8,128)(2,1)} %refs_3_.1), channel_id=1, source_target_pairs={{0,1},{1,0},{2,3},{3,2},{4,5},{5,4},{6,7},{7,6},{8,9},{9,8},{10,11... | collective-permute-start | bytes 98312 | tf_op jit(solution)/shard_map/ppermute | solution.py:41
  6.4 1.6 %collective-permute-start = (bf16[16,8,128]{2,1,0:T(8,128)(2,1)}, bf16[16,8,128]{2,1,0:T(8,128)(2,1)S(1)}, u32[]{:S(2)}, u32[]{:S(2)}) collective-permute-start(bf16[16,8,128]{2,1,0:T(8,128)(2,1)} %refs_3_.1), channel_id=1, source_target_pairs={{0,8},{4,12},{8,0},{12,4},{16,24},{20,28},{24,16},{28,20},{1,9},{5... | collective-permute-start | bytes 98312 | tf_op jit(solution)/shard_map/ppermute | solution.py:41
  8.0 1.5 %collective-permute-start.1 = (bf16[16,8,128]{2,1,0:T(8,128)(2,1)}, bf16[16,8,128]{2,1,0:T(8,128)(2,1)S(1)}, u32[]{:S(2)}, u32[]{:S(2)}) collective-permute-start(bf16[16,8,128]{2,1,0:T(8,128)(2,1)} %refs_3_.1), channel_id=1, source_target_pairs={{0,16},{4,20},{8,24},{12,28},{16,0},{20,4},{24,8},{28,12},{1,17},{... | collective-permute-start | bytes 98312 | tf_op jit(solution)/shard_map/ppermute | solution.py:41
  9.6 0.0 collective-permute-done.3.refs_0_
  9.6 1.0 %collective-permute-start.2 = (bf16[16,8,128]{2,1,0:T(8,128)(2,1)}, bf16[16,8,128]{2,1,0:T(8,128)(2,1)S(1)}, u32[]{:S(2)}, u32[]{:S(2)}) collective-permute-start(bf16[16,8,128]{2,1,0:T(8,128)(2,1)} %refs_3_.1), channel_id=1, source_target_pairs={{0,24},{4,28},{8,16},{12,20},{16,8},{20,12},{24,0},{28,4},{1,25},{... | collective-permute-start | bytes 98312 | tf_op jit(solution)/shard_map/ppermute | solution.py:41
  10.6 0.2 collective-permute-done.4.refs_1_
  10.8 0.0 collective-permute-done.5.refs_2_
  10.8 0.1 assemble.3.rest
  10.8 2.5 %collective-permute-start.7 = (bf16[24,16,128]{2,1,0:T(8,128)(2,1)S(1)}, bf16[24,16,128]{2,1,0:T(8,128)(2,1)S(1)}, u32[]{:S(2)}, u32[]{:S(2)}) collective-permute-start(bf16[24,16,128]{2,1,0:T(8,128)(2,1)S(1)} %assemble.3.rest), channel_id=1, source_target_pairs={{0,24},{4,28},{8,16},{12,20},{16,8},{20,12},{24,0},{28,4},{1,25},{... | collective-permute-start | bytes 294920 | tf_op jit(solution)/shard_map/ppermute | solution.py:41
  13.3 0.5 %collective-permute-start.9 = (bf16[24,16,128]{2,1,0:T(8,128)(2,1)S(1)}, bf16[24,16,128]{2,1,0:T(8,128)(2,1)S(1)}, u32[]{:S(2)}, u32[]{:S(2)}) collective-permute-start(bf16[24,16,128]{2,1,0:T(8,128)(2,1)S(1)} %assemble.3.rest), channel_id=1, source_target_pairs={{0,8},{4,12},{8,0},{12,4},{16,24},{20,28},{24,16},{28,20},{1,9},{5... | collective-permute-start | bytes 294920 | tf_op jit(solution)/shard_map/ppermute | solution.py:41
  13.9 0.0 collective-permute-done.refs_0_
  13.9 0.5 %collective-permute-start.6 = (bf16[24,16,128]{2,1,0:T(8,128)(2,1)S(1)}, bf16[24,16,128]{2,1,0:T(8,128)(2,1)S(1)}, u32[]{:S(2)}, u32[]{:S(2)}) collective-permute-start(bf16[24,16,128]{2,1,0:T(8,128)(2,1)S(1)} %assemble.3.rest), channel_id=1, source_target_pairs={{0,16},{4,20},{8,24},{12,28},{16,0},{20,4},{24,8},{28,12},{1,17},{... | collective-permute-start | bytes 294920 | tf_op jit(solution)/shard_map/ppermute | solution.py:41
  14.4 0.0 collective-permute-done.1.refs_1_
  14.4 0.5 %collective-permute-done.2.refs_2_ = bf16[16,8,128]{2,1,0:T(8,128)(2,1)S(1)} collective-permute-done((bf16[16,8,128]{2,1,0:T(8,128)(2,1)}, bf16[16,8,128]{2,1,0:T(8,128)(2,1)S(1)}, u32[]{:S(2)}, u32[]{:S(2)}) %collective-permute-start.2) | collective-permute-done | bytes 32800 | tf_op jit(solution)/shard_map/ppermute | solution.py:41
  14.9 0.0 copy-done.3
  14.9 0.1 assemble.2.token
  15.0 0.0 copy-start.1
  15.0 0.0 copy-start.2
  15.1 0.0 copy-start
  15.1 0.1 collective-permute-start.11
  15.2 0.6 %spread.1 = (f32[4,32,8,128]{3,2,1,0:T(8,128)S(1)}, f32[4,32,8,128]{3,2,1,0:T(8,128)S(1)}, f32[4,128]{1,0:T(4,128)S(1)}) custom-call(bf16[32,16,128]{2,1,0:T(8,128)(2,1)S(1)} %join.4.column), custom_call_target="tpu_custom_call" | custom-call | flops 1024000 | tf_op jit(solution)/shard_map/spread/pallas_call | solution.py:103
  15.7 0.2 copy-done.1
  15.9 0.0 copy-done.2
  15.9 0.1 copy-done
  16.0 0.6 %filter.4 = (f32[4,32,8,128]{3,2,1,0:T(8,128)S(1)}, f32[4,32,8,128]{3,2,1,0:T(8,128)S(1)}, f32[4,128]{1,0:T(4,128)S(1)}) custom-call(bf16[256,256]{1,0:T(8,128)(2,1)S(1)} %copy-done, bf16[256,256]{1,0:T(8,128)(2,1)S(1)} %copy-done.1, bf16[128,256]{1,0:T(8,128)(2,1)S(1)} %copy-done.2, f32[4,32,8,128]{3,2,1,0:T(8,128)S(1)} %get-tuple-element.14.refs_3_, ...), custom_call_target="tpu_custom_call" | custom-call | flops 8388608 | tf_op jit(solution)/shard_map/filter/pallas_call | solution.py:285
  16.7 0.0 collective-permute-done.7.rest
  16.7 0.3 %collective-permute-start.12 = (bf16[32,16,128]{2,1,0:T(8,128)(2,1)S(1)}, bf16[32,16,128]{2,1,0:T(8,128)(2,1)S(1)}, u32[]{:S(2)}, u32[]{:S(2)}) collective-permute-start(bf16[32,16,128]{2,1,0:T(8,128)(2,1)S(1)} %join.5), channel_id=1, source_target_pairs={{0,4},{4,0},{8,12},{12,8},{16,20},{20,16},{24,28},{28,24},{1,5},{5... | collective-permute-start | bytes 393224 | tf_op jit(solution)/shard_map/ppermute | solution.py:41
  17.0 0.7 %filter.5 = (f32[4,32,8,128]{3,2,1,0:T(8,128)S(1)}, f32[4,32,8,128]{3,2,1,0:T(8,128)S(1)}, f32[4,128]{1,0:T(4,128)S(1)}) custom-call(bf16[256,256]{1,0:T(8,128)(2,1)S(1)} %copy-done, bf16[256,256]{1,0:T(8,128)(2,1)S(1)} %copy-done.1, bf16[128,256]{1,0:T(8,128)(2,1)S(1)} %copy-done.2, f32[4,32,8,128]{3,2,1,0:T(8,128)S(1)} %get-tuple-element.14.refs_3_, ...), custom_call_target="tpu_custom_call" | custom-call | flops 8388608 | tf_op jit(solution)/shard_map/filter/pallas_call | solution.py:285
  17.6 0.3 %collective-permute-done.9.rest = bf16[24,16,128]{2,1,0:T(8,128)(2,1)S(1)} collective-permute-done((bf16[24,16,128]{2,1,0:T(8,128)(2,1)S(1)}, bf16[24,16,128]{2,1,0:T(8,128)(2,1)S(1)}, u32[]{:S(2)}, u32[]{:S(2)}) %collective-permute-start.9) | collective-permute-done | bytes 98336 | tf_op jit(solution)/shard_map/ppermute | solution.py:41
  18.0 0.1 collective-permute-start.10
  18.1 0.4 %collective-permute-done.6.rest = bf16[24,16,128]{2,1,0:T(8,128)(2,1)S(1)} collective-permute-done((bf16[24,16,128]{2,1,0:T(8,128)(2,1)S(1)}, bf16[24,16,128]{2,1,0:T(8,128)(2,1)S(1)}, u32[]{:S(2)}, u32[]{:S(2)}) %collective-permute-start.6) | collective-permute-done | bytes 98336 | tf_op jit(solution)/shard_map/ppermute | solution.py:41
  18.5 0.1 collective-permute-start.8
  18.6 0.0 collective-permute-done.11
  18.6 0.0 collective-permute-done.12
  18.6 1.6 %filter.6 = (f32[4,32,8,128]{3,2,1,0:T(8,128)S(1)}, f32[4,32,8,128]{3,2,1,0:T(8,128)S(1)}, f32[4,128]{1,0:T(4,128)S(1)}) custom-call(bf16[256,256]{1,0:T(8,128)(2,1)S(1)} %copy-done, bf16[256,256]{1,0:T(8,128)(2,1)S(1)} %copy-done.1, bf16[128,256]{1,0:T(8,128)(2,1)S(1)} %copy-done.2, f32[4,32,8,128]{3,2,1,0:T(8,128)S(1)} %get-tuple-element.14.refs_3_, ...), custom_call_target="tpu_custom_call" | custom-call | flops 33554432 | tf_op jit(solution)/shard_map/filter/pallas_call | solution.py:285
  20.3 0.0 collective-permute-done.10
  20.3 0.0 collective-permute-done.8
  20.3 1.8 %filter.7 = (f32[4,32,128]{2,1,0:T(8,128)}, f32[4]{0:T(128)}) custom-call(bf16[256,256]{1,0:T(8,128)(2,1)S(1)} %copy-done, bf16[256,256]{1,0:T(8,128)(2,1)S(1)} %copy-done.1, bf16[128,256]{1,0:T(8,128)(2,1)S(1)} %copy-done.2, f32[4,32,8,128]{3,2,1,0:T(8,128)S(1)} %get-tuple-element.14.refs_3_, f32[4,32,8,128]{3,2,1,0:T(8,128)S(1)} %get-tuple-element.15.refs_4_, ...), custom_call_target="tpu_custom_call" | custom-call | flops 16777216 | tf_op jit(solution)/shard_map/filter/pallas_call | solution.py:285
  (5 shorter events, 0.1 us)
Async XLA Ops:
  0.6 14.3 %copy-start.3 = (bf16[16,8,128]{2,1,0:T(8,128)(2,1)S(1)}, bf16[16,8,128]{2,1,0:T(8,128)(2,1)}, u32[]{:S(2)}) copy-start(bf16[16,8,128]{2,1,0:T(8,128)(2,1)} %refs_3_.1) | copy-start | bytes 98308
  0.6 8.9 %collective-permute-start.3 = (bf16[16,8,128]{2,1,0:T(8,128)(2,1)}, bf16[16,8,128]{2,1,0:T(8,128)(2,1)S(1)}, u32[]{:S(2)}, u32[]{:S(2)}) collective-permute-start(bf16[16,8,128]{2,1,0:T(8,128)(2,1)} %refs_3_.1), channel_id=1, source_target_pairs={{0,3},{1,2},{2,1},{3,0},{4,7},{5,6},{6,5},{7,4},{8,11},{9,10},{10,... | collective-permute-start | bytes 98312 | tf_op jit(solution)/shard_map/ppermute | solution.py:41
  5.8 5.0 %collective-permute-start.4 = (bf16[16,8,128]{2,1,0:T(8,128)(2,1)}, bf16[16,8,128]{2,1,0:T(8,128)(2,1)S(1)}, u32[]{:S(2)}, u32[]{:S(2)}) collective-permute-start(bf16[16,8,128]{2,1,0:T(8,128)(2,1)} %refs_3_.1), channel_id=1, source_target_pairs={{0,2},{1,3},{2,0},{3,1},{4,6},{5,7},{6,4},{7,5},{8,10},{9,11},{10,... | collective-permute-start | bytes 98312 | tf_op jit(solution)/shard_map/ppermute | solution.py:41
  5.8 5.0 %collective-permute-start.5 = (bf16[16,8,128]{2,1,0:T(8,128)(2,1)}, bf16[16,8,128]{2,1,0:T(8,128)(2,1)S(1)}, u32[]{:S(2)}, u32[]{:S(2)}) collective-permute-start(bf16[16,8,128]{2,1,0:T(8,128)(2,1)} %refs_3_.1), channel_id=1, source_target_pairs={{0,1},{1,0},{2,3},{3,2},{4,5},{5,4},{6,7},{7,6},{8,9},{9,8},{10,11... | collective-permute-start | bytes 98312 | tf_op jit(solution)/shard_map/ppermute | solution.py:41
  6.4 7.5 %collective-permute-start = (bf16[16,8,128]{2,1,0:T(8,128)(2,1)}, bf16[16,8,128]{2,1,0:T(8,128)(2,1)S(1)}, u32[]{:S(2)}, u32[]{:S(2)}) collective-permute-start(bf16[16,8,128]{2,1,0:T(8,128)(2,1)} %refs_3_.1), channel_id=1, source_target_pairs={{0,8},{4,12},{8,0},{12,4},{16,24},{20,28},{24,16},{28,20},{1,9},{5... | collective-permute-start | bytes 98312 | tf_op jit(solution)/shard_map/ppermute | solution.py:41
  8.0 6.4 %collective-permute-start.1 = (bf16[16,8,128]{2,1,0:T(8,128)(2,1)}, bf16[16,8,128]{2,1,0:T(8,128)(2,1)S(1)}, u32[]{:S(2)}, u32[]{:S(2)}) collective-permute-start(bf16[16,8,128]{2,1,0:T(8,128)(2,1)} %refs_3_.1), channel_id=1, source_target_pairs={{0,16},{4,20},{8,24},{12,28},{16,0},{20,4},{24,8},{28,12},{1,17},{... | collective-permute-start | bytes 98312 | tf_op jit(solution)/shard_map/ppermute | solution.py:41
  9.6 5.4 %collective-permute-start.2 = (bf16[16,8,128]{2,1,0:T(8,128)(2,1)}, bf16[16,8,128]{2,1,0:T(8,128)(2,1)S(1)}, u32[]{:S(2)}, u32[]{:S(2)}) collective-permute-start(bf16[16,8,128]{2,1,0:T(8,128)(2,1)} %refs_3_.1), channel_id=1, source_target_pairs={{0,24},{4,28},{8,16},{12,20},{16,8},{20,12},{24,0},{28,4},{1,25},{... | collective-permute-start | bytes 98312 | tf_op jit(solution)/shard_map/ppermute | solution.py:41
  10.8 5.8 %collective-permute-start.7 = (bf16[24,16,128]{2,1,0:T(8,128)(2,1)S(1)}, bf16[24,16,128]{2,1,0:T(8,128)(2,1)S(1)}, u32[]{:S(2)}, u32[]{:S(2)}) collective-permute-start(bf16[24,16,128]{2,1,0:T(8,128)(2,1)S(1)} %assemble.3.rest), channel_id=1, source_target_pairs={{0,24},{4,28},{8,16},{12,20},{16,8},{20,12},{24,0},{28,4},{1,25},{... | collective-permute-start | bytes 294920 | tf_op jit(solution)/shard_map/ppermute | solution.py:41
  13.3 4.6 %collective-permute-start.9 = (bf16[24,16,128]{2,1,0:T(8,128)(2,1)S(1)}, bf16[24,16,128]{2,1,0:T(8,128)(2,1)S(1)}, u32[]{:S(2)}, u32[]{:S(2)}) collective-permute-start(bf16[24,16,128]{2,1,0:T(8,128)(2,1)S(1)} %assemble.3.rest), channel_id=1, source_target_pairs={{0,8},{4,12},{8,0},{12,4},{16,24},{20,28},{24,16},{28,20},{1,9},{5... | collective-permute-start | bytes 294920 | tf_op jit(solution)/shard_map/ppermute | solution.py:41
  13.9 4.6 %collective-permute-start.6 = (bf16[24,16,128]{2,1,0:T(8,128)(2,1)S(1)}, bf16[24,16,128]{2,1,0:T(8,128)(2,1)S(1)}, u32[]{:S(2)}, u32[]{:S(2)}) collective-permute-start(bf16[24,16,128]{2,1,0:T(8,128)(2,1)S(1)} %assemble.3.rest), channel_id=1, source_target_pairs={{0,16},{4,20},{8,24},{12,28},{16,0},{20,4},{24,8},{28,12},{1,17},{... | collective-permute-start | bytes 294920 | tf_op jit(solution)/shard_map/ppermute | solution.py:41
  15.0 0.9 %copy-start.1 = (bf16[256,256]{1,0:T(8,128)(2,1)S(1)}, bf16[256,256]{1,0:T(8,128)(2,1)}, u32[]{:S(2)}) copy-start(bf16[256,256]{1,0:T(8,128)(2,1)} %constant.7.clone.refs_1_) | copy-start | bytes 393220
  15.0 0.9 %copy-start.2 = (bf16[128,256]{1,0:T(8,128)(2,1)S(1)}, bf16[128,256]{1,0:T(8,128)(2,1)}, u32[]{:S(2)}) copy-start(bf16[128,256]{1,0:T(8,128)(2,1)} %constant.8.clone.refs_2_) | copy-start | bytes 196612
  15.1 1.0 %copy-start = (bf16[256,256]{1,0:T(8,128)(2,1)S(1)}, bf16[256,256]{1,0:T(8,128)(2,1)}, u32[]{:S(2)}) copy-start(bf16[256,256]{1,0:T(8,128)(2,1)} %constant.6.clone.refs_0_) | copy-start | bytes 393220
  15.1 3.6 %collective-permute-start.11 = (bf16[32,16,128]{2,1,0:T(8,128)(2,1)S(1)}, bf16[32,16,128]{2,1,0:T(8,128)(2,1)S(1)}, u32[]{:S(2)}, u32[]{:S(2)}) collective-permute-start(bf16[32,16,128]{2,1,0:T(8,128)(2,1)S(1)} %join.4.column), channel_id=1, source_target_pairs={{0,4},{4,0},{8,12},{12,8},{16,20},{20,16},{24,28},{28,24},{1,5},{5... | collective-permute-start | bytes 393224 | tf_op jit(solution)/shard_map/ppermute | solution.py:41
  16.7 1.9 %collective-permute-start.12 = (bf16[32,16,128]{2,1,0:T(8,128)(2,1)S(1)}, bf16[32,16,128]{2,1,0:T(8,128)(2,1)S(1)}, u32[]{:S(2)}, u32[]{:S(2)}) collective-permute-start(bf16[32,16,128]{2,1,0:T(8,128)(2,1)S(1)} %join.5), channel_id=1, source_target_pairs={{0,4},{4,0},{8,12},{12,8},{16,20},{20,16},{24,28},{28,24},{1,5},{5... | collective-permute-start | bytes 393224 | tf_op jit(solution)/shard_map/ppermute | solution.py:41
  18.0 2.3 %collective-permute-start.10 = (bf16[32,16,128]{2,1,0:T(8,128)(2,1)S(1)}, bf16[32,16,128]{2,1,0:T(8,128)(2,1)S(1)}, u32[]{:S(2)}, u32[]{:S(2)}) collective-permute-start(bf16[32,16,128]{2,1,0:T(8,128)(2,1)S(1)} %join.7), channel_id=1, source_target_pairs={{0,4},{4,0},{8,12},{12,8},{16,20},{20,16},{24,28},{28,24},{1,5},{5... | collective-permute-start | bytes 393224 | tf_op jit(solution)/shard_map/ppermute | solution.py:41
  18.5 1.8 %collective-permute-start.8 = (bf16[32,16,128]{2,1,0:T(8,128)(2,1)S(1)}, bf16[32,16,128]{2,1,0:T(8,128)(2,1)S(1)}, u32[]{:S(2)}, u32[]{:S(2)}) collective-permute-start(bf16[32,16,128]{2,1,0:T(8,128)(2,1)S(1)} %join.6), channel_id=1, source_target_pairs={{0,4},{4,0},{8,12},{12,8},{16,20},{20,16},{24,28},{28,24},{1,5},{5... | collective-permute-start | bytes 393224 | tf_op jit(solution)/shard_map/ppermute | solution.py:41

commit v4 on v3

--- a/solution.py
+++ b/solution.py
@@ -243,7 +243,7 @@
                 imag_sum[i, places[n]] = totals[n][1][i]
         return carry
 
-    lax.fori_loop(0, radial // 2, filtered, 0, unroll=2)
+    lax.fori_loop(0, radial // 2, filtered, 0, unroll=True)
 
     if is_last:
         for k in range(ranges):

time: 22.3 us -> 22 us (0.987)
  Pallas kernels: 5.44 us -> 5.04 us
    pallas_call x4, Pallas kernels: 4.73 us -> 4.33 us  [filter_stage(): pl.pallas_call(functools.partial(filter_kernel, ranges, slice_place, len(...]
where the time goes in v4:
time: 22 us; the launch traced here: 21.8 us
  starting transfers between devices  14 us (64%)
  Pallas kernels  5.04 us (23%)
  waiting for transfers between devices  1.6 us (7%)
  between operations  0.78 us (4%)
  local copies, waits for them, and re-layouts  0.35 us (2%)
    ppermute x13, starting transfers between devices, moved(): return lax.ppermute(array, axis, pairs)  14 us
    pallas_call x4, Pallas kernels, filter_stage(): pl.pallas_call(functools.partial(filter_kernel, ranges, slice_place, len(...  4.33 us
    ppermute x13, waiting for transfers between devices, moved(): return lax.ppermute(array, axis, pairs)  1.6 us
    pallas_call x1, Pallas kernels, spread_own(): small_kernel(functools.partial(spread_kernel, ranges), (tiles, tiles, jax...  0.56 us
  transfers between devices with their start and end apart: 13, of which 4 were waited for; matrix products, arithmetic and copies ran while one was open for 0% of the time, Pallas kernels for 16%

profile of v4, /device:TPU:0, one launch (start us, length us, event | category | flops | bytes accessed | tf_op | source)
XLA Modules:
  0.0 21.8 jit_solution(14322294621141657702)
XLA Ops:
  0.6 0.0 copy-start.3
  0.6 5.1 %collective-permute-start.3 = (bf16[16,8,128]{2,1,0:T(8,128)(2,1)}, bf16[16,8,128]{2,1,0:T(8,128)(2,1)S(1)}, u32[]{:S(2)}, u32[]{:S(2)}) collective-permute-start(bf16[16,8,128]{2,1,0:T(8,128)(2,1)} %refs_3_.1), channel_id=1, source_target_pairs={{0,3},{1,2},{2,1},{3,0},{4,7},{5,6},{6,5},{7,4},{8,11},{9,10},{10,... | collective-permute-start | bytes 98312 | tf_op jit(solution)/shard_map/ppermute | solution.py:41
  5.8 0.0 collective-permute-start.4
  5.8 0.6 %collective-permute-start.5 = (bf16[16,8,128]{2,1,0:T(8,128)(2,1)}, bf16[16,8,128]{2,1,0:T(8,128)(2,1)S(1)}, u32[]{:S(2)}, u32[]{:S(2)}) collective-permute-start(bf16[16,8,128]{2,1,0:T(8,128)(2,1)} %refs_3_.1), channel_id=1, source_target_pairs={{0,1},{1,0},{2,3},{3,2},{4,5},{5,4},{6,7},{7,6},{8,9},{9,8},{10,11... | collective-permute-start | bytes 98312 | tf_op jit(solution)/shard_map/ppermute | solution.py:41
  6.4 1.6 %collective-permute-start = (bf16[16,8,128]{2,1,0:T(8,128)(2,1)}, bf16[16,8,128]{2,1,0:T(8,128)(2,1)S(1)}, u32[]{:S(2)}, u32[]{:S(2)}) collective-permute-start(bf16[16,8,128]{2,1,0:T(8,128)(2,1)} %refs_3_.1), channel_id=1, source_target_pairs={{0,8},{4,12},{8,0},{12,4},{16,24},{20,28},{24,16},{28,20},{1,9},{5... | collective-permute-start | bytes 98312 | tf_op jit(solution)/shard_map/ppermute | solution.py:41
  8.0 1.5 %collective-permute-start.1 = (bf16[16,8,128]{2,1,0:T(8,128)(2,1)}, bf16[16,8,128]{2,1,0:T(8,128)(2,1)S(1)}, u32[]{:S(2)}, u32[]{:S(2)}) collective-permute-start(bf16[16,8,128]{2,1,0:T(8,128)(2,1)} %refs_3_.1), channel_id=1, source_target_pairs={{0,16},{4,20},{8,24},{12,28},{16,0},{20,4},{24,8},{28,12},{1,17},{... | collective-permute-start | bytes 98312 | tf_op jit(solution)/shard_map/ppermute | solution.py:41
  9.6 0.0 collective-permute-done.3.refs_0_
  9.6 1.0 %collective-permute-start.2 = (bf16[16,8,128]{2,1,0:T(8,128)(2,1)}, bf16[16,8,128]{2,1,0:T(8,128)(2,1)S(1)}, u32[]{:S(2)}, u32[]{:S(2)}) collective-permute-start(bf16[16,8,128]{2,1,0:T(8,128)(2,1)} %refs_3_.1), channel_id=1, source_target_pairs={{0,24},{4,28},{8,16},{12,20},{16,8},{20,12},{24,0},{28,4},{1,25},{... | collective-permute-start | bytes 98312 | tf_op jit(solution)/shard_map/ppermute | solution.py:41
  10.6 0.2 collective-permute-done.4.refs_1_
  10.8 0.0 collective-permute-done.5.refs_2_
  10.8 0.1 assemble.3.rest
  10.8 2.5 %collective-permute-start.7 = (bf16[24,16,128]{2,1,0:T(8,128)(2,1)S(1)}, bf16[24,16,128]{2,1,0:T(8,128)(2,1)S(1)}, u32[]{:S(2)}, u32[]{:S(2)}) collective-permute-start(bf16[24,16,128]{2,1,0:T(8,128)(2,1)S(1)} %assemble.3.rest), channel_id=1, source_target_pairs={{0,24},{4,28},{8,16},{12,20},{16,8},{20,12},{24,0},{28,4},{1,25},{... | collective-permute-start | bytes 294920 | tf_op jit(solution)/shard_map/ppermute | solution.py:41
  13.3 0.5 %collective-permute-start.9 = (bf16[24,16,128]{2,1,0:T(8,128)(2,1)S(1)}, bf16[24,16,128]{2,1,0:T(8,128)(2,1)S(1)}, u32[]{:S(2)}, u32[]{:S(2)}) collective-permute-start(bf16[24,16,128]{2,1,0:T(8,128)(2,1)S(1)} %assemble.3.rest), channel_id=1, source_target_pairs={{0,8},{4,12},{8,0},{12,4},{16,24},{20,28},{24,16},{28,20},{1,9},{5... | collective-permute-start | bytes 294920 | tf_op jit(solution)/shard_map/ppermute | solution.py:41
  13.9 0.0 collective-permute-done.refs_0_
  13.9 0.5 %collective-permute-start.6 = (bf16[24,16,128]{2,1,0:T(8,128)(2,1)S(1)}, bf16[24,16,128]{2,1,0:T(8,128)(2,1)S(1)}, u32[]{:S(2)}, u32[]{:S(2)}) collective-permute-start(bf16[24,16,128]{2,1,0:T(8,128)(2,1)S(1)} %assemble.3.rest), channel_id=1, source_target_pairs={{0,16},{4,20},{8,24},{12,28},{16,0},{20,4},{24,8},{28,12},{1,17},{... | collective-permute-start | bytes 294920 | tf_op jit(solution)/shard_map/ppermute | solution.py:41
  14.4 0.0 collective-permute-done.1.refs_1_
  14.4 0.5 %collective-permute-done.2.refs_2_ = bf16[16,8,128]{2,1,0:T(8,128)(2,1)S(1)} collective-permute-done((bf16[16,8,128]{2,1,0:T(8,128)(2,1)}, bf16[16,8,128]{2,1,0:T(8,128)(2,1)S(1)}, u32[]{:S(2)}, u32[]{:S(2)}) %collective-permute-start.2) | collective-permute-done | bytes 32800 | tf_op jit(solution)/shard_map/ppermute | solution.py:41
  14.9 0.0 copy-done.3
  14.9 0.1 assemble.2.token
  15.0 0.0 copy-start.1
  15.0 0.0 copy-start.2
  15.1 0.0 copy-start
  15.1 0.1 collective-permute-start.11
  15.2 0.6 %spread.1 = (f32[4,32,8,128]{3,2,1,0:T(8,128)S(1)}, f32[4,32,8,128]{3,2,1,0:T(8,128)S(1)}, f32[4,128]{1,0:T(4,128)S(1)}) custom-call(bf16[32,16,128]{2,1,0:T(8,128)(2,1)S(1)} %join.4.column), custom_call_target="tpu_custom_call" | custom-call | flops 1024000 | tf_op jit(solution)/shard_map/spread/pallas_call | solution.py:103
  15.7 0.2 copy-done.1
  15.9 0.0 copy-done.2
  15.9 0.1 copy-done
  16.0 0.6 %filter.4 = (f32[4,32,8,128]{3,2,1,0:T(8,128)S(1)}, f32[4,32,8,128]{3,2,1,0:T(8,128)S(1)}, f32[4,128]{1,0:T(4,128)S(1)}) custom-call(bf16[256,256]{1,0:T(8,128)(2,1)S(1)} %copy-done, bf16[256,256]{1,0:T(8,128)(2,1)S(1)} %copy-done.1, bf16[128,256]{1,0:T(8,128)(2,1)S(1)} %copy-done.2, f32[4,32,8,128]{3,2,1,0:T(8,128)S(1)} %get-tuple-element.14.refs_3_, ...), custom_call_target="tpu_custom_call" | custom-call | flops 8388608 | tf_op jit(solution)/shard_map/filter/pallas_call | solution.py:285
  16.6 0.0 collective-permute-done.7.rest
  16.7 0.3 %collective-permute-start.12 = (bf16[32,16,128]{2,1,0:T(8,128)(2,1)S(1)}, bf16[32,16,128]{2,1,0:T(8,128)(2,1)S(1)}, u32[]{:S(2)}, u32[]{:S(2)}) collective-permute-start(bf16[32,16,128]{2,1,0:T(8,128)(2,1)S(1)} %join.5), channel_id=1, source_target_pairs={{0,4},{4,0},{8,12},{12,8},{16,20},{20,16},{24,28},{28,24},{1,5},{5... | collective-permute-start | bytes 393224 | tf_op jit(solution)/shard_map/ppermute | solution.py:41
  16.9 0.6 %filter.5 = (f32[4,32,8,128]{3,2,1,0:T(8,128)S(1)}, f32[4,32,8,128]{3,2,1,0:T(8,128)S(1)}, f32[4,128]{1,0:T(4,128)S(1)}) custom-call(bf16[256,256]{1,0:T(8,128)(2,1)S(1)} %copy-done, bf16[256,256]{1,0:T(8,128)(2,1)S(1)} %copy-done.1, bf16[128,256]{1,0:T(8,128)(2,1)S(1)} %copy-done.2, f32[4,32,8,128]{3,2,1,0:T(8,128)S(1)} %get-tuple-element.14.refs_3_, ...), custom_call_target="tpu_custom_call" | custom-call | flops 8388608 | tf_op jit(solution)/shard_map/filter/pallas_call | solution.py:285
  17.5 0.4 %collective-permute-done.9.rest = bf16[24,16,128]{2,1,0:T(8,128)(2,1)S(1)} collective-permute-done((bf16[24,16,128]{2,1,0:T(8,128)(2,1)S(1)}, bf16[24,16,128]{2,1,0:T(8,128)(2,1)S(1)}, u32[]{:S(2)}, u32[]{:S(2)}) %collective-permute-start.9) | collective-permute-done | bytes 98336 | tf_op jit(solution)/shard_map/ppermute | solution.py:41
  18.0 0.1 collective-permute-start.10
  18.1 0.4 %collective-permute-done.6.rest = bf16[24,16,128]{2,1,0:T(8,128)(2,1)S(1)} collective-permute-done((bf16[24,16,128]{2,1,0:T(8,128)(2,1)S(1)}, bf16[24,16,128]{2,1,0:T(8,128)(2,1)S(1)}, u32[]{:S(2)}, u32[]{:S(2)}) %collective-permute-start.6) | collective-permute-done | bytes 98336 | tf_op jit(solution)/shard_map/ppermute | solution.py:41
  18.5 0.1 collective-permute-start.8
  18.6 0.0 collective-permute-done.11
  18.6 0.0 collective-permute-done.12
  18.6 1.5 %filter.6 = (f32[4,32,8,128]{3,2,1,0:T(8,128)S(1)}, f32[4,32,8,128]{3,2,1,0:T(8,128)S(1)}, f32[4,128]{1,0:T(4,128)S(1)}) custom-call(bf16[256,256]{1,0:T(8,128)(2,1)S(1)} %copy-done, bf16[256,256]{1,0:T(8,128)(2,1)S(1)} %copy-done.1, bf16[128,256]{1,0:T(8,128)(2,1)S(1)} %copy-done.2, f32[4,32,8,128]{3,2,1,0:T(8,128)S(1)} %get-tuple-element.14.refs_3_, ...), custom_call_target="tpu_custom_call" | custom-call | flops 33554432 | tf_op jit(solution)/shard_map/filter/pallas_call | solution.py:285
  20.1 0.0 collective-permute-done.10
  20.1 0.0 collective-permute-done.8
  20.1 1.7 %filter.7 = (f32[4,32,128]{2,1,0:T(8,128)}, f32[4]{0:T(128)}) custom-call(bf16[256,256]{1,0:T(8,128)(2,1)S(1)} %copy-done, bf16[256,256]{1,0:T(8,128)(2,1)S(1)} %copy-done.1, bf16[128,256]{1,0:T(8,128)(2,1)S(1)} %copy-done.2, f32[4,32,8,128]{3,2,1,0:T(8,128)S(1)} %get-tuple-element.14.refs_3_, f32[4,32,8,128]{3,2,1,0:T(8,128)S(1)} %get-tuple-element.15.refs_4_, ...), custom_call_target="tpu_custom_call" | custom-call | flops 16777216 | tf_op jit(solution)/shard_map/filter/pallas_call | solution.py:285
  (5 shorter events, 0.1 us)
Async XLA Ops:
  0.6 14.3 %copy-start.3 = (bf16[16,8,128]{2,1,0:T(8,128)(2,1)S(1)}, bf16[16,8,128]{2,1,0:T(8,128)(2,1)}, u32[]{:S(2)}) copy-start(bf16[16,8,128]{2,1,0:T(8,128)(2,1)} %refs_3_.1) | copy-start | bytes 98308
  0.6 8.9 %collective-permute-start.3 = (bf16[16,8,128]{2,1,0:T(8,128)(2,1)}, bf16[16,8,128]{2,1,0:T(8,128)(2,1)S(1)}, u32[]{:S(2)}, u32[]{:S(2)}) collective-permute-start(bf16[16,8,128]{2,1,0:T(8,128)(2,1)} %refs_3_.1), channel_id=1, source_target_pairs={{0,3},{1,2},{2,1},{3,0},{4,7},{5,6},{6,5},{7,4},{8,11},{9,10},{10,... | collective-permute-start | bytes 98312 | tf_op jit(solution)/shard_map/ppermute | solution.py:41
  5.8 5.0 %collective-permute-start.4 = (bf16[16,8,128]{2,1,0:T(8,128)(2,1)}, bf16[16,8,128]{2,1,0:T(8,128)(2,1)S(1)}, u32[]{:S(2)}, u32[]{:S(2)}) collective-permute-start(bf16[16,8,128]{2,1,0:T(8,128)(2,1)} %refs_3_.1), channel_id=1, source_target_pairs={{0,2},{1,3},{2,0},{3,1},{4,6},{5,7},{6,4},{7,5},{8,10},{9,11},{10,... | collective-permute-start | bytes 98312 | tf_op jit(solution)/shard_map/ppermute | solution.py:41
  5.8 5.0 %collective-permute-start.5 = (bf16[16,8,128]{2,1,0:T(8,128)(2,1)}, bf16[16,8,128]{2,1,0:T(8,128)(2,1)S(1)}, u32[]{:S(2)}, u32[]{:S(2)}) collective-permute-start(bf16[16,8,128]{2,1,0:T(8,128)(2,1)} %refs_3_.1), channel_id=1, source_target_pairs={{0,1},{1,0},{2,3},{3,2},{4,5},{5,4},{6,7},{7,6},{8,9},{9,8},{10,11... | collective-permute-start | bytes 98312 | tf_op jit(solution)/shard_map/ppermute | solution.py:41
  6.4 7.5 %collective-permute-start = (bf16[16,8,128]{2,1,0:T(8,128)(2,1)}, bf16[16,8,128]{2,1,0:T(8,128)(2,1)S(1)}, u32[]{:S(2)}, u32[]{:S(2)}) collective-permute-start(bf16[16,8,128]{2,1,0:T(8,128)(2,1)} %refs_3_.1), channel_id=1, source_target_pairs={{0,8},{4,12},{8,0},{12,4},{16,24},{20,28},{24,16},{28,20},{1,9},{5... | collective-permute-start | bytes 98312 | tf_op jit(solution)/shard_map/ppermute | solution.py:41
  8.0 6.4 %collective-permute-start.1 = (bf16[16,8,128]{2,1,0:T(8,128)(2,1)}, bf16[16,8,128]{2,1,0:T(8,128)(2,1)S(1)}, u32[]{:S(2)}, u32[]{:S(2)}) collective-permute-start(bf16[16,8,128]{2,1,0:T(8,128)(2,1)} %refs_3_.1), channel_id=1, source_target_pairs={{0,16},{4,20},{8,24},{12,28},{16,0},{20,4},{24,8},{28,12},{1,17},{... | collective-permute-start | bytes 98312 | tf_op jit(solution)/shard_map/ppermute | solution.py:41
  9.6 5.4 %collective-permute-start.2 = (bf16[16,8,128]{2,1,0:T(8,128)(2,1)}, bf16[16,8,128]{2,1,0:T(8,128)(2,1)S(1)}, u32[]{:S(2)}, u32[]{:S(2)}) collective-permute-start(bf16[16,8,128]{2,1,0:T(8,128)(2,1)} %refs_3_.1), channel_id=1, source_target_pairs={{0,24},{4,28},{8,16},{12,20},{16,8},{20,12},{24,0},{28,4},{1,25},{... | collective-permute-start | bytes 98312 | tf_op jit(solution)/shard_map/ppermute | solution.py:41
  10.8 5.8 %collective-permute-start.7 = (bf16[24,16,128]{2,1,0:T(8,128)(2,1)S(1)}, bf16[24,16,128]{2,1,0:T(8,128)(2,1)S(1)}, u32[]{:S(2)}, u32[]{:S(2)}) collective-permute-start(bf16[24,16,128]{2,1,0:T(8,128)(2,1)S(1)} %assemble.3.rest), channel_id=1, source_target_pairs={{0,24},{4,28},{8,16},{12,20},{16,8},{20,12},{24,0},{28,4},{1,25},{... | collective-permute-start | bytes 294920 | tf_op jit(solution)/shard_map/ppermute | solution.py:41
  13.3 4.6 %collective-permute-start.9 = (bf16[24,16,128]{2,1,0:T(8,128)(2,1)S(1)}, bf16[24,16,128]{2,1,0:T(8,128)(2,1)S(1)}, u32[]{:S(2)}, u32[]{:S(2)}) collective-permute-start(bf16[24,16,128]{2,1,0:T(8,128)(2,1)S(1)} %assemble.3.rest), channel_id=1, source_target_pairs={{0,8},{4,12},{8,0},{12,4},{16,24},{20,28},{24,16},{28,20},{1,9},{5... | collective-permute-start | bytes 294920 | tf_op jit(solution)/shard_map/ppermute | solution.py:41
  13.9 4.6 %collective-permute-start.6 = (bf16[24,16,128]{2,1,0:T(8,128)(2,1)S(1)}, bf16[24,16,128]{2,1,0:T(8,128)(2,1)S(1)}, u32[]{:S(2)}, u32[]{:S(2)}) collective-permute-start(bf16[24,16,128]{2,1,0:T(8,128)(2,1)S(1)} %assemble.3.rest), channel_id=1, source_target_pairs={{0,16},{4,20},{8,24},{12,28},{16,0},{20,4},{24,8},{28,12},{1,17},{... | collective-permute-start | bytes 294920 | tf_op jit(solution)/shard_map/ppermute | solution.py:41
  15.0 0.9 %copy-start.1 = (bf16[256,256]{1,0:T(8,128)(2,1)S(1)}, bf16[256,256]{1,0:T(8,128)(2,1)}, u32[]{:S(2)}) copy-start(bf16[256,256]{1,0:T(8,128)(2,1)} %constant.7.clone.refs_1_) | copy-start | bytes 393220
  15.0 0.9 %copy-start.2 = (bf16[128,256]{1,0:T(8,128)(2,1)S(1)}, bf16[128,256]{1,0:T(8,128)(2,1)}, u32[]{:S(2)}) copy-start(bf16[128,256]{1,0:T(8,128)(2,1)} %constant.8.clone.refs_2_) | copy-start | bytes 196612
  15.1 1.0 %copy-start = (bf16[256,256]{1,0:T(8,128)(2,1)S(1)}, bf16[256,256]{1,0:T(8,128)(2,1)}, u32[]{:S(2)}) copy-start(bf16[256,256]{1,0:T(8,128)(2,1)} %constant.6.clone.refs_0_) | copy-start | bytes 393220
  15.1 3.6 %collective-permute-start.11 = (bf16[32,16,128]{2,1,0:T(8,128)(2,1)S(1)}, bf16[32,16,128]{2,1,0:T(8,128)(2,1)S(1)}, u32[]{:S(2)}, u32[]{:S(2)}) collective-permute-start(bf16[32,16,128]{2,1,0:T(8,128)(2,1)S(1)} %join.4.column), channel_id=1, source_target_pairs={{0,4},{4,0},{8,12},{12,8},{16,20},{20,16},{24,28},{28,24},{1,5},{5... | collective-permute-start | bytes 393224 | tf_op jit(solution)/shard_map/ppermute | solution.py:41
  16.7 2.0 %collective-permute-start.12 = (bf16[32,16,128]{2,1,0:T(8,128)(2,1)S(1)}, bf16[32,16,128]{2,1,0:T(8,128)(2,1)S(1)}, u32[]{:S(2)}, u32[]{:S(2)}) collective-permute-start(bf16[32,16,128]{2,1,0:T(8,128)(2,1)S(1)} %join.5), channel_id=1, source_target_pairs={{0,4},{4,0},{8,12},{12,8},{16,20},{20,16},{24,28},{28,24},{1,5},{5... | collective-permute-start | bytes 393224 | tf_op jit(solution)/shard_map/ppermute | solution.py:41
  18.0 2.1 %collective-permute-start.10 = (bf16[32,16,128]{2,1,0:T(8,128)(2,1)S(1)}, bf16[32,16,128]{2,1,0:T(8,128)(2,1)S(1)}, u32[]{:S(2)}, u32[]{:S(2)}) collective-permute-start(bf16[32,16,128]{2,1,0:T(8,128)(2,1)S(1)} %join.7), channel_id=1, source_target_pairs={{0,4},{4,0},{8,12},{12,8},{16,20},{20,16},{24,28},{28,24},{1,5},{5... | collective-permute-start | bytes 393224 | tf_op jit(solution)/shard_map/ppermute | solution.py:41
  18.5 1.6 %collective-permute-start.8 = (bf16[32,16,128]{2,1,0:T(8,128)(2,1)S(1)}, bf16[32,16,128]{2,1,0:T(8,128)(2,1)S(1)}, u32[]{:S(2)}, u32[]{:S(2)}) collective-permute-start(bf16[32,16,128]{2,1,0:T(8,128)(2,1)S(1)} %join.6), channel_id=1, source_target_pairs={{0,4},{4,0},{8,12},{12,8},{16,20},{20,16},{24,28},{28,24},{1,5},{5... | collective-permute-start | bytes 393224 | tf_op jit(solution)/shard_map/ppermute | solution.py:41

commit v5 on v4

--- a/solution.py
+++ b/solution.py
@@ -328,8 +328,9 @@
     depth = local.shape[1]
     far = range(lax.axis_size("blk") - 2, 0, -2)
     slices = [flipped(local, "off", k) for k in range(lax.axis_size("off") - 1, 0, -1)]
-    heads = assemble([flipped(local, "blk", flip) for flip in far][::-1] + [local])
+    heads = assemble([flipped(local, "blk", flip) for flip in far] + [local])
     head = [heads[n * depth : (n + 1) * depth] for n in range(len(far) + 1)]
+    head = head[:1] + head[:0:-1]
     rest = assemble(slices)
     rests = [flipped(rest, "blk", flip) for flip in far]
     column = join(head[0], rest, heads)
@@ -339,7 +340,7 @@
     carry = run(carry, [first], False)
     others = [join(h, r, carry[2]) for h, r in zip(head[2:], rests[1:])]
     twins = [flipped(block, "blk", 1) for block in [column, first] + others]
-    carry = run(carry, others + twins[:2], not others)
+    carry = run(carry, twins[:2] + others, not others)
     return run(carry, twins[2:], True) if others else carry
 
 

time: 22 us -> 22 us (level)
  starting transfers between devices: 14 us -> 13.1 us
  waiting for transfers between devices: 1.6 us -> 2.5 us
    ppermute x13, starting transfers between devices: 14 us -> 13.1 us  [moved(): return lax.ppermute(array, axis, pairs)]
    ppermute x13, waiting for transfers between devices: 1.6 us -> 2.5 us  [moved(): return lax.ppermute(array, axis, pairs)]
where the time goes in v5:
time: 22 us; the launch traced here: 21.8 us
  starting transfers between devices  13.1 us (60%)
  Pallas kernels  5.05 us (23%)
  waiting for transfers between devices  2.5 us (11%)
  between operations  0.78 us (4%)
  local copies, waits for them, and re-layouts  0.35 us (2%)
    ppermute x13, starting transfers between devices, moved(): return lax.ppermute(array, axis, pairs)  13.1 us
    pallas_call x4, Pallas kernels, filter_stage(): pl.pallas_call(functools.partial(filter_kernel, ranges, slice_place, len(...  4.33 us
    ppermute x13, waiting for transfers between devices, moved(): return lax.ppermute(array, axis, pairs)  2.5 us
    pallas_call x1, Pallas kernels, spread_own(): small_kernel(functools.partial(spread_kernel, ranges), (tiles, tiles, jax...  0.56 us
  transfers between devices with their start and end apart: 13, of which 4 were waited for; matrix products, arithmetic and copies ran while one was open for 0% of the time, Pallas kernels for 16%

profile of v5, /device:TPU:0, one launch (start us, length us, event | category | flops | bytes accessed | tf_op | source)
XLA Modules:
  0.0 21.8 jit_solution(42806375420896253)
XLA Ops:
  0.6 0.0 copy-start.3
  0.6 5.1 %collective-permute-start.3 = (bf16[16,8,128]{2,1,0:T(8,128)(2,1)}, bf16[16,8,128]{2,1,0:T(8,128)(2,1)S(1)}, u32[]{:S(2)}, u32[]{:S(2)}) collective-permute-start(bf16[16,8,128]{2,1,0:T(8,128)(2,1)} %refs_3_.1), channel_id=1, source_target_pairs={{0,3},{1,2},{2,1},{3,0},{4,7},{5,6},{6,5},{7,4},{8,11},{9,10},{10,... | collective-permute-start | bytes 98312 | tf_op jit(solution)/shard_map/ppermute | solution.py:41
  5.8 0.0 collective-permute-start.4
  5.8 0.6 %collective-permute-start.5 = (bf16[16,8,128]{2,1,0:T(8,128)(2,1)}, bf16[16,8,128]{2,1,0:T(8,128)(2,1)S(1)}, u32[]{:S(2)}, u32[]{:S(2)}) collective-permute-start(bf16[16,8,128]{2,1,0:T(8,128)(2,1)} %refs_3_.1), channel_id=1, source_target_pairs={{0,1},{1,0},{2,3},{3,2},{4,5},{5,4},{6,7},{7,6},{8,9},{9,8},{10,11... | collective-permute-start | bytes 98312 | tf_op jit(solution)/shard_map/ppermute | solution.py:41
  6.4 2.6 %collective-permute-start = (bf16[16,8,128]{2,1,0:T(8,128)(2,1)}, bf16[16,8,128]{2,1,0:T(8,128)(2,1)S(1)}, u32[]{:S(2)}, u32[]{:S(2)}) collective-permute-start(bf16[16,8,128]{2,1,0:T(8,128)(2,1)} %refs_3_.1), channel_id=1, source_target_pairs={{0,24},{4,28},{8,16},{12,20},{16,8},{20,12},{24,0},{28,4},{1,25},{... | collective-permute-start | bytes 98312 | tf_op jit(solution)/shard_map/ppermute | solution.py:41
  9.0 0.5 %collective-permute-start.1 = (bf16[16,8,128]{2,1,0:T(8,128)(2,1)}, bf16[16,8,128]{2,1,0:T(8,128)(2,1)S(1)}, u32[]{:S(2)}, u32[]{:S(2)}) collective-permute-start(bf16[16,8,128]{2,1,0:T(8,128)(2,1)} %refs_3_.1), channel_id=1, source_target_pairs={{0,16},{4,20},{8,24},{12,28},{16,0},{20,4},{24,8},{28,12},{1,17},{... | collective-permute-start | bytes 98312 | tf_op jit(solution)/shard_map/ppermute | solution.py:41
  9.5 0.0 collective-permute-done.3.refs_0_
  9.5 0.4 %collective-permute-start.2 = (bf16[16,8,128]{2,1,0:T(8,128)(2,1)}, bf16[16,8,128]{2,1,0:T(8,128)(2,1)S(1)}, u32[]{:S(2)}, u32[]{:S(2)}) collective-permute-start(bf16[16,8,128]{2,1,0:T(8,128)(2,1)} %refs_3_.1), channel_id=1, source_target_pairs={{0,8},{4,12},{8,0},{12,4},{16,24},{20,28},{24,16},{28,20},{1,9},{5... | collective-permute-start | bytes 98312 | tf_op jit(solution)/shard_map/ppermute | solution.py:41
  9.9 0.9 %collective-permute-done.4.refs_1_ = bf16[16,8,128]{2,1,0:T(8,128)(2,1)S(1)} collective-permute-done((bf16[16,8,128]{2,1,0:T(8,128)(2,1)}, bf16[16,8,128]{2,1,0:T(8,128)(2,1)S(1)}, u32[]{:S(2)}, u32[]{:S(2)}) %collective-permute-start.4) | collective-permute-done | bytes 32800 | tf_op jit(solution)/shard_map/ppermute | solution.py:41
  10.8 0.0 collective-permute-done.5.refs_2_
  10.8 0.1 assemble.3.rest
  10.8 2.5 %collective-permute-start.7 = (bf16[24,16,128]{2,1,0:T(8,128)(2,1)S(1)}, bf16[24,16,128]{2,1,0:T(8,128)(2,1)S(1)}, u32[]{:S(2)}, u32[]{:S(2)}) collective-permute-start(bf16[24,16,128]{2,1,0:T(8,128)(2,1)S(1)} %assemble.3.rest), channel_id=1, source_target_pairs={{0,24},{4,28},{8,16},{12,20},{16,8},{20,12},{24,0},{28,4},{1,25},{... | collective-permute-start | bytes 294920 | tf_op jit(solution)/shard_map/ppermute | solution.py:41
  13.3 0.5 %collective-permute-start.9 = (bf16[24,16,128]{2,1,0:T(8,128)(2,1)S(1)}, bf16[24,16,128]{2,1,0:T(8,128)(2,1)S(1)}, u32[]{:S(2)}, u32[]{:S(2)}) collective-permute-start(bf16[24,16,128]{2,1,0:T(8,128)(2,1)S(1)} %assemble.3.rest), channel_id=1, source_target_pairs={{0,8},{4,12},{8,0},{12,4},{16,24},{20,28},{24,16},{28,20},{1,9},{5... | collective-permute-start | bytes 294920 | tf_op jit(solution)/shard_map/ppermute | solution.py:41
  13.9 0.0 collective-permute-done.refs_0_
  13.9 0.5 %collective-permute-start.6 = (bf16[24,16,128]{2,1,0:T(8,128)(2,1)S(1)}, bf16[24,16,128]{2,1,0:T(8,128)(2,1)S(1)}, u32[]{:S(2)}, u32[]{:S(2)}) collective-permute-start(bf16[24,16,128]{2,1,0:T(8,128)(2,1)S(1)} %assemble.3.rest), channel_id=1, source_target_pairs={{0,16},{4,20},{8,24},{12,28},{16,0},{20,4},{24,8},{28,12},{1,17},{... | collective-permute-start | bytes 294920 | tf_op jit(solution)/shard_map/ppermute | solution.py:41
  14.4 0.0 collective-permute-done.1.refs_1_
  14.4 0.0 collective-permute-done.2.refs_2_
  14.4 0.0 copy-done.3
  14.4 0.1 assemble.2.token
  14.5 0.0 copy-start.1
  14.5 0.0 copy-start.2
  14.5 0.0 copy-start
  14.6 0.1 collective-permute-start.11
  14.6 0.6 %spread.1 = (f32[4,32,8,128]{3,2,1,0:T(8,128)S(1)}, f32[4,32,8,128]{3,2,1,0:T(8,128)S(1)}, f32[4,128]{1,0:T(4,128)S(1)}) custom-call(bf16[32,16,128]{2,1,0:T(8,128)(2,1)S(1)} %join.4.column), custom_call_target="tpu_custom_call" | custom-call | flops 1024000 | tf_op jit(solution)/shard_map/spread/pallas_call | solution.py:103
  15.2 0.2 copy-done.1
  15.4 0.0 copy-done.2
  15.4 0.1 copy-done
  15.5 0.6 %filter.4 = (f32[4,32,8,128]{3,2,1,0:T(8,128)S(1)}, f32[4,32,8,128]{3,2,1,0:T(8,128)S(1)}, f32[4,128]{1,0:T(4,128)S(1)}) custom-call(bf16[256,256]{1,0:T(8,128)(2,1)S(1)} %copy-done, bf16[256,256]{1,0:T(8,128)(2,1)S(1)} %copy-done.1, bf16[128,256]{1,0:T(8,128)(2,1)S(1)} %copy-done.2, f32[4,32,8,128]{3,2,1,0:T(8,128)S(1)} %get-tuple-element.14.refs_3_, ...), custom_call_target="tpu_custom_call" | custom-call | flops 8388608 | tf_op jit(solution)/shard_map/filter/pallas_call | solution.py:285
  16.1 0.4 %collective-permute-done.7.rest = bf16[24,16,128]{2,1,0:T(8,128)(2,1)S(1)} collective-permute-done((bf16[24,16,128]{2,1,0:T(8,128)(2,1)S(1)}, bf16[24,16,128]{2,1,0:T(8,128)(2,1)S(1)}, u32[]{:S(2)}, u32[]{:S(2)}) %collective-permute-start.7) | collective-permute-done | bytes 98336 | tf_op jit(solution)/shard_map/ppermute | solution.py:41
  16.5 0.1 collective-permute-start.12
  16.6 0.6 %filter.5 = (f32[4,32,8,128]{3,2,1,0:T(8,128)S(1)}, f32[4,32,8,128]{3,2,1,0:T(8,128)S(1)}, f32[4,128]{1,0:T(4,128)S(1)}) custom-call(bf16[256,256]{1,0:T(8,128)(2,1)S(1)} %copy-done, bf16[256,256]{1,0:T(8,128)(2,1)S(1)} %copy-done.1, bf16[128,256]{1,0:T(8,128)(2,1)S(1)} %copy-done.2, f32[4,32,8,128]{3,2,1,0:T(8,128)S(1)} %get-tuple-element.14.refs_3_, ...), custom_call_target="tpu_custom_call" | custom-call | flops 8388608 | tf_op jit(solution)/shard_map/filter/pallas_call | solution.py:285
  17.2 0.8 %collective-permute-done.9.rest = bf16[24,16,128]{2,1,0:T(8,128)(2,1)S(1)} collective-permute-done((bf16[24,16,128]{2,1,0:T(8,128)(2,1)S(1)}, bf16[24,16,128]{2,1,0:T(8,128)(2,1)S(1)}, u32[]{:S(2)}, u32[]{:S(2)}) %collective-permute-start.9) | collective-permute-done | bytes 98336 | tf_op jit(solution)/shard_map/ppermute | solution.py:41
  18.0 0.1 collective-permute-start.10
  18.1 0.4 %collective-permute-done.6.rest = bf16[24,16,128]{2,1,0:T(8,128)(2,1)S(1)} collective-permute-done((bf16[24,16,128]{2,1,0:T(8,128)(2,1)S(1)}, bf16[24,16,128]{2,1,0:T(8,128)(2,1)S(1)}, u32[]{:S(2)}, u32[]{:S(2)}) %collective-permute-start.6) | collective-permute-done | bytes 98336 | tf_op jit(solution)/shard_map/ppermute | solution.py:41
  18.5 0.1 collective-permute-start.8
  18.6 0.0 collective-permute-done.11
  18.6 0.0 collective-permute-done.12
  18.6 1.5 %filter.6 = (f32[4,32,8,128]{3,2,1,0:T(8,128)S(1)}, f32[4,32,8,128]{3,2,1,0:T(8,128)S(1)}, f32[4,128]{1,0:T(4,128)S(1)}) custom-call(bf16[256,256]{1,0:T(8,128)(2,1)S(1)} %copy-done, bf16[256,256]{1,0:T(8,128)(2,1)S(1)} %copy-done.1, bf16[128,256]{1,0:T(8,128)(2,1)S(1)} %copy-done.2, f32[4,32,8,128]{3,2,1,0:T(8,128)S(1)} %get-tuple-element.14.refs_3_, ...), custom_call_target="tpu_custom_call" | custom-call | flops 33554432 | tf_op jit(solution)/shard_map/filter/pallas_call | solution.py:285
  20.1 0.0 collective-permute-done.10
  20.1 0.0 collective-permute-done.8
  20.1 1.7 %filter.7 = (f32[4,32,128]{2,1,0:T(8,128)}, f32[4]{0:T(128)}) custom-call(bf16[256,256]{1,0:T(8,128)(2,1)S(1)} %copy-done, bf16[256,256]{1,0:T(8,128)(2,1)S(1)} %copy-done.1, bf16[128,256]{1,0:T(8,128)(2,1)S(1)} %copy-done.2, f32[4,32,8,128]{3,2,1,0:T(8,128)S(1)} %get-tuple-element.14.refs_3_, f32[4,32,8,128]{3,2,1,0:T(8,128)S(1)} %get-tuple-element.15.refs_4_, ...), custom_call_target="tpu_custom_call" | custom-call | flops 16777216 | tf_op jit(solution)/shard_map/filter/pallas_call | solution.py:285
  (5 shorter events, 0.1 us)
Async XLA Ops:
  0.6 13.8 %copy-start.3 = (bf16[16,8,128]{2,1,0:T(8,128)(2,1)S(1)}, bf16[16,8,128]{2,1,0:T(8,128)(2,1)}, u32[]{:S(2)}) copy-start(bf16[16,8,128]{2,1,0:T(8,128)(2,1)} %refs_3_.1) | copy-start | bytes 98308
  0.6 8.9 %collective-permute-start.3 = (bf16[16,8,128]{2,1,0:T(8,128)(2,1)}, bf16[16,8,128]{2,1,0:T(8,128)(2,1)S(1)}, u32[]{:S(2)}, u32[]{:S(2)}) collective-permute-start(bf16[16,8,128]{2,1,0:T(8,128)(2,1)} %refs_3_.1), channel_id=1, source_target_pairs={{0,3},{1,2},{2,1},{3,0},{4,7},{5,6},{6,5},{7,4},{8,11},{9,10},{10,... | collective-permute-start | bytes 98312 | tf_op jit(solution)/shard_map/ppermute | solution.py:41
  5.8 5.0 %collective-permute-start.4 = (bf16[16,8,128]{2,1,0:T(8,128)(2,1)}, bf16[16,8,128]{2,1,0:T(8,128)(2,1)S(1)}, u32[]{:S(2)}, u32[]{:S(2)}) collective-permute-start(bf16[16,8,128]{2,1,0:T(8,128)(2,1)} %refs_3_.1), channel_id=1, source_target_pairs={{0,2},{1,3},{2,0},{3,1},{4,6},{5,7},{6,4},{7,5},{8,10},{9,11},{10,... | collective-permute-start | bytes 98312 | tf_op jit(solution)/shard_map/ppermute | solution.py:41
  5.8 5.0 %collective-permute-start.5 = (bf16[16,8,128]{2,1,0:T(8,128)(2,1)}, bf16[16,8,128]{2,1,0:T(8,128)(2,1)S(1)}, u32[]{:S(2)}, u32[]{:S(2)}) collective-permute-start(bf16[16,8,128]{2,1,0:T(8,128)(2,1)} %refs_3_.1), channel_id=1, source_target_pairs={{0,1},{1,0},{2,3},{3,2},{4,5},{5,4},{6,7},{7,6},{8,9},{9,8},{10,11... | collective-permute-start | bytes 98312 | tf_op jit(solution)/shard_map/ppermute | solution.py:41
  6.4 7.5 %collective-permute-start = (bf16[16,8,128]{2,1,0:T(8,128)(2,1)}, bf16[16,8,128]{2,1,0:T(8,128)(2,1)S(1)}, u32[]{:S(2)}, u32[]{:S(2)}) collective-permute-start(bf16[16,8,128]{2,1,0:T(8,128)(2,1)} %refs_3_.1), channel_id=1, source_target_pairs={{0,24},{4,28},{8,16},{12,20},{16,8},{20,12},{24,0},{28,4},{1,25},{... | collective-permute-start | bytes 98312 | tf_op jit(solution)/shard_map/ppermute | solution.py:41
  9.0 5.4 %collective-permute-start.1 = (bf16[16,8,128]{2,1,0:T(8,128)(2,1)}, bf16[16,8,128]{2,1,0:T(8,128)(2,1)S(1)}, u32[]{:S(2)}, u32[]{:S(2)}) collective-permute-start(bf16[16,8,128]{2,1,0:T(8,128)(2,1)} %refs_3_.1), channel_id=1, source_target_pairs={{0,16},{4,20},{8,24},{12,28},{16,0},{20,4},{24,8},{28,12},{1,17},{... | collective-permute-start | bytes 98312 | tf_op jit(solution)/shard_map/ppermute | solution.py:41
  9.5 4.9 %collective-permute-start.2 = (bf16[16,8,128]{2,1,0:T(8,128)(2,1)}, bf16[16,8,128]{2,1,0:T(8,128)(2,1)S(1)}, u32[]{:S(2)}, u32[]{:S(2)}) collective-permute-start(bf16[16,8,128]{2,1,0:T(8,128)(2,1)} %refs_3_.1), channel_id=1, source_target_pairs={{0,8},{4,12},{8,0},{12,4},{16,24},{20,28},{24,16},{28,20},{1,9},{5... | collective-permute-start | bytes 98312 | tf_op jit(solution)/shard_map/ppermute | solution.py:41
  10.8 5.6 %collective-permute-start.7 = (bf16[24,16,128]{2,1,0:T(8,128)(2,1)S(1)}, bf16[24,16,128]{2,1,0:T(8,128)(2,1)S(1)}, u32[]{:S(2)}, u32[]{:S(2)}) collective-permute-start(bf16[24,16,128]{2,1,0:T(8,128)(2,1)S(1)} %assemble.3.rest), channel_id=1, source_target_pairs={{0,24},{4,28},{8,16},{12,20},{16,8},{20,12},{24,0},{28,4},{1,25},{... | collective-permute-start | bytes 294920 | tf_op jit(solution)/shard_map/ppermute | solution.py:41
  13.3 4.6 %collective-permute-start.9 = (bf16[24,16,128]{2,1,0:T(8,128)(2,1)S(1)}, bf16[24,16,128]{2,1,0:T(8,128)(2,1)S(1)}, u32[]{:S(2)}, u32[]{:S(2)}) collective-permute-start(bf16[24,16,128]{2,1,0:T(8,128)(2,1)S(1)} %assemble.3.rest), channel_id=1, source_target_pairs={{0,8},{4,12},{8,0},{12,4},{16,24},{20,28},{24,16},{28,20},{1,9},{5... | collective-permute-start | bytes 294920 | tf_op jit(solution)/shard_map/ppermute | solution.py:41
  13.9 4.6 %collective-permute-start.6 = (bf16[24,16,128]{2,1,0:T(8,128)(2,1)S(1)}, bf16[24,16,128]{2,1,0:T(8,128)(2,1)S(1)}, u32[]{:S(2)}, u32[]{:S(2)}) collective-permute-start(bf16[24,16,128]{2,1,0:T(8,128)(2,1)S(1)} %assemble.3.rest), channel_id=1, source_target_pairs={{0,16},{4,20},{8,24},{12,28},{16,0},{20,4},{24,8},{28,12},{1,17},{... | collective-permute-start | bytes 294920 | tf_op jit(solution)/shard_map/ppermute | solution.py:41
  14.5 0.9 %copy-start.1 = (bf16[256,256]{1,0:T(8,128)(2,1)S(1)}, bf16[256,256]{1,0:T(8,128)(2,1)}, u32[]{:S(2)}) copy-start(bf16[256,256]{1,0:T(8,128)(2,1)} %constant.7.clone.refs_1_) | copy-start | bytes 393220
  14.5 0.9 %copy-start.2 = (bf16[128,256]{1,0:T(8,128)(2,1)S(1)}, bf16[128,256]{1,0:T(8,128)(2,1)}, u32[]{:S(2)}) copy-start(bf16[128,256]{1,0:T(8,128)(2,1)} %constant.8.clone.refs_2_) | copy-start | bytes 196612
  14.5 1.0 %copy-start = (bf16[256,256]{1,0:T(8,128)(2,1)S(1)}, bf16[256,256]{1,0:T(8,128)(2,1)}, u32[]{:S(2)}) copy-start(bf16[256,256]{1,0:T(8,128)(2,1)} %constant.6.clone.refs_0_) | copy-start | bytes 393220
  14.6 4.1 %collective-permute-start.11 = (bf16[32,16,128]{2,1,0:T(8,128)(2,1)S(1)}, bf16[32,16,128]{2,1,0:T(8,128)(2,1)S(1)}, u32[]{:S(2)}, u32[]{:S(2)}) collective-permute-start(bf16[32,16,128]{2,1,0:T(8,128)(2,1)S(1)} %join.4.column), channel_id=1, source_target_pairs={{0,4},{4,0},{8,12},{12,8},{16,20},{20,16},{24,28},{28,24},{1,5},{5... | collective-permute-start | bytes 393224 | tf_op jit(solution)/shard_map/ppermute | solution.py:41
  16.5 2.2 %collective-permute-start.12 = (bf16[32,16,128]{2,1,0:T(8,128)(2,1)S(1)}, bf16[32,16,128]{2,1,0:T(8,128)(2,1)S(1)}, u32[]{:S(2)}, u32[]{:S(2)}) collective-permute-start(bf16[32,16,128]{2,1,0:T(8,128)(2,1)S(1)} %join.5), channel_id=1, source_target_pairs={{0,4},{4,0},{8,12},{12,8},{16,20},{20,16},{24,28},{28,24},{1,5},{5... | collective-permute-start | bytes 393224 | tf_op jit(solution)/shard_map/ppermute | solution.py:41
  18.0 2.1 %collective-permute-start.10 = (bf16[32,16,128]{2,1,0:T(8,128)(2,1)S(1)}, bf16[32,16,128]{2,1,0:T(8,128)(2,1)S(1)}, u32[]{:S(2)}, u32[]{:S(2)}) collective-permute-start(bf16[32,16,128]{2,1,0:T(8,128)(2,1)S(1)} %join.7), channel_id=1, source_target_pairs={{0,4},{4,0},{8,12},{12,8},{16,20},{20,16},{24,28},{28,24},{1,5},{5... | collective-permute-start | bytes 393224 | tf_op jit(solution)/shard_map/ppermute | solution.py:41
  18.5 1.6 %collective-permute-start.8 = (bf16[32,16,128]{2,1,0:T(8,128)(2,1)S(1)}, bf16[32,16,128]{2,1,0:T(8,128)(2,1)S(1)}, u32[]{:S(2)}, u32[]{:S(2)}) collective-permute-start(bf16[32,16,128]{2,1,0:T(8,128)(2,1)S(1)} %join.6), channel_id=1, source_target_pairs={{0,4},{4,0},{8,12},{12,8},{16,20},{20,16},{24,28},{28,24},{1,5},{5... | collective-permute-start | bytes 393224 | tf_op jit(solution)/shard_map/ppermute | solution.py:41

commit v6 on v5

--- a/solution.py
+++ b/solution.py
@@ -298,18 +298,20 @@
     )(*operands)
 
 
-def assemble_kernel(*refs):
+def assemble_kernel(places, *refs):
     *slices, out, wide = refs
     depth = slices[0].shape[1]
-    for k, piece in enumerate(slices[::-1]):
-        radial_first(piece, wide, out, k * depth)
-
-
-def assemble(slices):
+    for place, piece in zip(places, slices):
+        radial_first(piece, wide, out, place * depth)
+
+
+def assemble(slices, places=None):
+    places = places or range(len(slices) - 1, -1, -1)
+    kernel = functools.partial(assemble_kernel, tuple(places))
     images, depth, angular = slices[0].shape
     whole = jax.ShapeDtypeStruct((len(slices) * depth, images, angular), slices[0].dtype)
     wide = [pltpu.VMEM((images * depth, angular), jnp.float32)]
-    return small_kernel(assemble_kernel, whole, len(slices), "assemble", 1 << 21, wide, 100)(*slices)
+    return small_kernel(kernel, whole, len(slices), "assemble", 1 << 21, wide, 100)(*slices)
 
 
 def join_kernel(first, rest, token, out):
@@ -327,11 +329,13 @@
 def by_flips(local, run):
     depth = local.shape[1]
     far = range(lax.axis_size("blk") - 2, 0, -2)
-    slices = [flipped(local, "off", k) for k in range(lax.axis_size("off") - 1, 0, -1)]
+    steps = list(range(lax.axis_size("off") - 1, 0, -1))
+    steps[:2] = steps[1::-1]
+    slices = [flipped(local, "off", k) for k in steps]
     heads = assemble([flipped(local, "blk", flip) for flip in far] + [local])
     head = [heads[n * depth : (n + 1) * depth] for n in range(len(far) + 1)]
     head = head[:1] + head[:0:-1]
-    rest = assemble(slices)
+    rest = assemble(slices, [k - 1 for k in steps])
     rests = [flipped(rest, "blk", flip) for flip in far]
     column = join(head[0], rest, heads)
     run = functools.partial(run, spread_own(column, lax.axis_size("off")))

time: 22 us -> 21.9 us (level)
  no operation moved by 1% of the time
where the time goes in v6:
time: 21.9 us; the launch traced here: 21.7 us
  starting transfers between devices  13.1 us (60%)
  Pallas kernels  5.05 us (23%)
  waiting for transfers between devices  2.46 us (11%)
  between operations  0.78 us (4%)
  local copies, waits for them, and re-layouts  0.35 us (2%)
    ppermute x13, starting transfers between devices, moved(): return lax.ppermute(array, axis, pairs)  13.1 us
    pallas_call x4, Pallas kernels, filter_stage(): pl.pallas_call(functools.partial(filter_kernel, ranges, slice_place, len(...  4.33 us
    ppermute x13, waiting for transfers between devices, moved(): return lax.ppermute(array, axis, pairs)  2.46 us
    pallas_call x1, Pallas kernels, spread_own(): small_kernel(functools.partial(spread_kernel, ranges), (tiles, tiles, jax...  0.56 us
  transfers between devices with their start and end apart: 13, of which 4 were waited for; matrix products, arithmetic and copies ran while one was open for 0% of the time, Pallas kernels for 16%

profile of v6, /device:TPU:0, one launch (start us, length us, event | category | flops | bytes accessed | tf_op | source)
XLA Modules:
  0.0 21.7 jit_solution(3272702557223469074)
XLA Ops:
  0.6 0.0 copy-start.3
  0.6 4.1 %collective-permute-start.3 = (bf16[16,8,128]{2,1,0:T(8,128)(2,1)}, bf16[16,8,128]{2,1,0:T(8,128)(2,1)S(1)}, u32[]{:S(2)}, u32[]{:S(2)}) collective-permute-start(bf16[16,8,128]{2,1,0:T(8,128)(2,1)} %refs_3_.1), channel_id=1, source_target_pairs={{0,2},{1,3},{2,0},{3,1},{4,6},{5,7},{6,4},{7,5},{8,10},{9,11},{10,... | collective-permute-start | bytes 98312 | tf_op jit(solution)/shard_map/ppermute | solution.py:41
  4.7 1.3 %collective-permute-start.4 = (bf16[16,8,128]{2,1,0:T(8,128)(2,1)}, bf16[16,8,128]{2,1,0:T(8,128)(2,1)S(1)}, u32[]{:S(2)}, u32[]{:S(2)}) collective-permute-start(bf16[16,8,128]{2,1,0:T(8,128)(2,1)} %refs_3_.1), channel_id=1, source_target_pairs={{0,3},{1,2},{2,1},{3,0},{4,7},{5,6},{6,5},{7,4},{8,11},{9,10},{10,... | collective-permute-start | bytes 98312 | tf_op jit(solution)/shard_map/ppermute | solution.py:41
  6.1 0.2 %collective-permute-start.5 = (bf16[16,8,128]{2,1,0:T(8,128)(2,1)}, bf16[16,8,128]{2,1,0:T(8,128)(2,1)S(1)}, u32[]{:S(2)}, u32[]{:S(2)}) collective-permute-start(bf16[16,8,128]{2,1,0:T(8,128)(2,1)} %refs_3_.1), channel_id=1, source_target_pairs={{0,1},{1,0},{2,3},{3,2},{4,5},{5,4},{6,7},{7,6},{8,9},{9,8},{10,11... | collective-permute-start | bytes 98312 | tf_op jit(solution)/shard_map/ppermute | solution.py:41
  6.3 2.4 %collective-permute-start = (bf16[16,8,128]{2,1,0:T(8,128)(2,1)}, bf16[16,8,128]{2,1,0:T(8,128)(2,1)S(1)}, u32[]{:S(2)}, u32[]{:S(2)}) collective-permute-start(bf16[16,8,128]{2,1,0:T(8,128)(2,1)} %refs_3_.1), channel_id=1, source_target_pairs={{0,24},{4,28},{8,16},{12,20},{16,8},{20,12},{24,0},{28,4},{1,25},{... | collective-permute-start | bytes 98312 | tf_op jit(solution)/shard_map/ppermute | solution.py:41
  8.8 0.5 %collective-permute-start.1 = (bf16[16,8,128]{2,1,0:T(8,128)(2,1)}, bf16[16,8,128]{2,1,0:T(8,128)(2,1)S(1)}, u32[]{:S(2)}, u32[]{:S(2)}) collective-permute-start(bf16[16,8,128]{2,1,0:T(8,128)(2,1)} %refs_3_.1), channel_id=1, source_target_pairs={{0,16},{4,20},{8,24},{12,28},{16,0},{20,4},{24,8},{28,12},{1,17},{... | collective-permute-start | bytes 98312 | tf_op jit(solution)/shard_map/ppermute | solution.py:41
  9.3 0.0 collective-permute-done.3.refs_0_
  9.3 0.5 %collective-permute-start.2 = (bf16[16,8,128]{2,1,0:T(8,128)(2,1)}, bf16[16,8,128]{2,1,0:T(8,128)(2,1)S(1)}, u32[]{:S(2)}, u32[]{:S(2)}) collective-permute-start(bf16[16,8,128]{2,1,0:T(8,128)(2,1)} %refs_3_.1), channel_id=1, source_target_pairs={{0,8},{4,12},{8,0},{12,4},{16,24},{20,28},{24,16},{28,20},{1,9},{5... | collective-permute-start | bytes 98312 | tf_op jit(solution)/shard_map/ppermute | solution.py:41
  9.8 0.8 %collective-permute-done.4.refs_1_ = bf16[16,8,128]{2,1,0:T(8,128)(2,1)S(1)} collective-permute-done((bf16[16,8,128]{2,1,0:T(8,128)(2,1)}, bf16[16,8,128]{2,1,0:T(8,128)(2,1)S(1)}, u32[]{:S(2)}, u32[]{:S(2)}) %collective-permute-start.4) | collective-permute-done | bytes 32800 | tf_op jit(solution)/shard_map/ppermute | solution.py:41
  10.7 0.0 collective-permute-done.5.refs_2_
  10.7 0.1 assemble.3.rest
  10.7 2.5 %collective-permute-start.7 = (bf16[24,16,128]{2,1,0:T(8,128)(2,1)S(1)}, bf16[24,16,128]{2,1,0:T(8,128)(2,1)S(1)}, u32[]{:S(2)}, u32[]{:S(2)}) collective-permute-start(bf16[24,16,128]{2,1,0:T(8,128)(2,1)S(1)} %assemble.3.rest), channel_id=1, source_target_pairs={{0,24},{4,28},{8,16},{12,20},{16,8},{20,12},{24,0},{28,4},{1,25},{... | collective-permute-start | bytes 294920 | tf_op jit(solution)/shard_map/ppermute | solution.py:41
  13.2 0.5 %collective-permute-start.9 = (bf16[24,16,128]{2,1,0:T(8,128)(2,1)S(1)}, bf16[24,16,128]{2,1,0:T(8,128)(2,1)S(1)}, u32[]{:S(2)}, u32[]{:S(2)}) collective-permute-start(bf16[24,16,128]{2,1,0:T(8,128)(2,1)S(1)} %assemble.3.rest), channel_id=1, source_target_pairs={{0,8},{4,12},{8,0},{12,4},{16,24},{20,28},{24,16},{28,20},{1,9},{5... | collective-permute-start | bytes 294920 | tf_op jit(solution)/shard_map/ppermute | solution.py:41
  13.8 0.0 collective-permute-done.refs_0_
  13.8 0.5 %collective-permute-start.6 = (bf16[24,16,128]{2,1,0:T(8,128)(2,1)S(1)}, bf16[24,16,128]{2,1,0:T(8,128)(2,1)S(1)}, u32[]{:S(2)}, u32[]{:S(2)}) collective-permute-start(bf16[24,16,128]{2,1,0:T(8,128)(2,1)S(1)} %assemble.3.rest), channel_id=1, source_target_pairs={{0,16},{4,20},{8,24},{12,28},{16,0},{20,4},{24,8},{28,12},{1,17},{... | collective-permute-start | bytes 294920 | tf_op jit(solution)/shard_map/ppermute | solution.py:41
  14.3 0.0 collective-permute-done.1.refs_1_
  14.3 0.0 collective-permute-done.2.refs_2_
  14.3 0.0 copy-done.3
  14.3 0.1 assemble.2.token
  14.4 0.0 copy-start.1
  14.4 0.0 copy-start.2
  14.4 0.0 copy-start
  14.4 0.1 collective-permute-start.11
  14.5 0.6 %spread.1 = (f32[4,32,8,128]{3,2,1,0:T(8,128)S(1)}, f32[4,32,8,128]{3,2,1,0:T(8,128)S(1)}, f32[4,128]{1,0:T(4,128)S(1)}) custom-call(bf16[32,16,128]{2,1,0:T(8,128)(2,1)S(1)} %join.4.column), custom_call_target="tpu_custom_call" | custom-call | flops 1024000 | tf_op jit(solution)/shard_map/spread/pallas_call | solution.py:103
  15.1 0.2 copy-done.1
  15.3 0.0 copy-done.2
  15.3 0.1 copy-done
  15.4 0.6 %filter.4 = (f32[4,32,8,128]{3,2,1,0:T(8,128)S(1)}, f32[4,32,8,128]{3,2,1,0:T(8,128)S(1)}, f32[4,128]{1,0:T(4,128)S(1)}) custom-call(bf16[256,256]{1,0:T(8,128)(2,1)S(1)} %copy-done, bf16[256,256]{1,0:T(8,128)(2,1)S(1)} %copy-done.1, bf16[128,256]{1,0:T(8,128)(2,1)S(1)} %copy-done.2, f32[4,32,8,128]{3,2,1,0:T(8,128)S(1)} %get-tuple-element.14.refs_3_, ...), custom_call_target="tpu_custom_call" | custom-call | flops 8388608 | tf_op jit(solution)/shard_map/filter/pallas_call | solution.py:285
  16.0 0.4 %collective-permute-done.7.rest = bf16[24,16,128]{2,1,0:T(8,128)(2,1)S(1)} collective-permute-done((bf16[24,16,128]{2,1,0:T(8,128)(2,1)S(1)}, bf16[24,16,128]{2,1,0:T(8,128)(2,1)S(1)}, u32[]{:S(2)}, u32[]{:S(2)}) %collective-permute-start.7) | collective-permute-done | bytes 98336 | tf_op jit(solution)/shard_map/ppermute | solution.py:41
  16.4 0.1 collective-permute-start.12
  16.4 0.6 %filter.5 = (f32[4,32,8,128]{3,2,1,0:T(8,128)S(1)}, f32[4,32,8,128]{3,2,1,0:T(8,128)S(1)}, f32[4,128]{1,0:T(4,128)S(1)}) custom-call(bf16[256,256]{1,0:T(8,128)(2,1)S(1)} %copy-done, bf16[256,256]{1,0:T(8,128)(2,1)S(1)} %copy-done.1, bf16[128,256]{1,0:T(8,128)(2,1)S(1)} %copy-done.2, f32[4,32,8,128]{3,2,1,0:T(8,128)S(1)} %get-tuple-element.14.refs_3_, ...), custom_call_target="tpu_custom_call" | custom-call | flops 8388608 | tf_op jit(solution)/shard_map/filter/pallas_call | solution.py:285
  17.1 0.8 %collective-permute-done.9.rest = bf16[24,16,128]{2,1,0:T(8,128)(2,1)S(1)} collective-permute-done((bf16[24,16,128]{2,1,0:T(8,128)(2,1)S(1)}, bf16[24,16,128]{2,1,0:T(8,128)(2,1)S(1)}, u32[]{:S(2)}, u32[]{:S(2)}) %collective-permute-start.9) | collective-permute-done | bytes 98336 | tf_op jit(solution)/shard_map/ppermute | solution.py:41
  17.9 0.1 collective-permute-start.10
  17.9 0.4 %collective-permute-done.6.rest = bf16[24,16,128]{2,1,0:T(8,128)(2,1)S(1)} collective-permute-done((bf16[24,16,128]{2,1,0:T(8,128)(2,1)S(1)}, bf16[24,16,128]{2,1,0:T(8,128)(2,1)S(1)}, u32[]{:S(2)}, u32[]{:S(2)}) %collective-permute-start.6) | collective-permute-done | bytes 98336 | tf_op jit(solution)/shard_map/ppermute | solution.py:41
  18.4 0.1 collective-permute-start.8
  18.5 0.0 collective-permute-done.11
  18.5 0.0 collective-permute-done.12
  18.5 1.5 %filter.6 = (f32[4,32,8,128]{3,2,1,0:T(8,128)S(1)}, f32[4,32,8,128]{3,2,1,0:T(8,128)S(1)}, f32[4,128]{1,0:T(4,128)S(1)}) custom-call(bf16[256,256]{1,0:T(8,128)(2,1)S(1)} %copy-done, bf16[256,256]{1,0:T(8,128)(2,1)S(1)} %copy-done.1, bf16[128,256]{1,0:T(8,128)(2,1)S(1)} %copy-done.2, f32[4,32,8,128]{3,2,1,0:T(8,128)S(1)} %get-tuple-element.14.refs_3_, ...), custom_call_target="tpu_custom_call" | custom-call | flops 33554432 | tf_op jit(solution)/shard_map/filter/pallas_call | solution.py:285
  20.0 0.0 collective-permute-done.10
  20.0 0.0 collective-permute-done.8
  20.0 1.7 %filter.7 = (f32[4,32,128]{2,1,0:T(8,128)}, f32[4]{0:T(128)}) custom-call(bf16[256,256]{1,0:T(8,128)(2,1)S(1)} %copy-done, bf16[256,256]{1,0:T(8,128)(2,1)S(1)} %copy-done.1, bf16[128,256]{1,0:T(8,128)(2,1)S(1)} %copy-done.2, f32[4,32,8,128]{3,2,1,0:T(8,128)S(1)} %get-tuple-element.14.refs_3_, f32[4,32,8,128]{3,2,1,0:T(8,128)S(1)} %get-tuple-element.15.refs_4_, ...), custom_call_target="tpu_custom_call" | custom-call | flops 16777216 | tf_op jit(solution)/shard_map/filter/pallas_call | solution.py:285
  (5 shorter events, 0.1 us)
Async XLA Ops:
  0.6 13.7 %copy-start.3 = (bf16[16,8,128]{2,1,0:T(8,128)(2,1)S(1)}, bf16[16,8,128]{2,1,0:T(8,128)(2,1)}, u32[]{:S(2)}) copy-start(bf16[16,8,128]{2,1,0:T(8,128)(2,1)} %refs_3_.1) | copy-start | bytes 98308
  0.6 8.6 %collective-permute-start.3 = (bf16[16,8,128]{2,1,0:T(8,128)(2,1)}, bf16[16,8,128]{2,1,0:T(8,128)(2,1)S(1)}, u32[]{:S(2)}, u32[]{:S(2)}) collective-permute-start(bf16[16,8,128]{2,1,0:T(8,128)(2,1)} %refs_3_.1), channel_id=1, source_target_pairs={{0,2},{1,3},{2,0},{3,1},{4,6},{5,7},{6,4},{7,5},{8,10},{9,11},{10,... | collective-permute-start | bytes 98312 | tf_op jit(solution)/shard_map/ppermute | solution.py:41
  4.7 5.9 %collective-permute-start.4 = (bf16[16,8,128]{2,1,0:T(8,128)(2,1)}, bf16[16,8,128]{2,1,0:T(8,128)(2,1)S(1)}, u32[]{:S(2)}, u32[]{:S(2)}) collective-permute-start(bf16[16,8,128]{2,1,0:T(8,128)(2,1)} %refs_3_.1), channel_id=1, source_target_pairs={{0,3},{1,2},{2,1},{3,0},{4,7},{5,6},{6,5},{7,4},{8,11},{9,10},{10,... | collective-permute-start | bytes 98312 | tf_op jit(solution)/shard_map/ppermute | solution.py:41
  6.1 4.6 %collective-permute-start.5 = (bf16[16,8,128]{2,1,0:T(8,128)(2,1)}, bf16[16,8,128]{2,1,0:T(8,128)(2,1)S(1)}, u32[]{:S(2)}, u32[]{:S(2)}) collective-permute-start(bf16[16,8,128]{2,1,0:T(8,128)(2,1)} %refs_3_.1), channel_id=1, source_target_pairs={{0,1},{1,0},{2,3},{3,2},{4,5},{5,4},{6,7},{7,6},{8,9},{9,8},{10,11... | collective-permute-start | bytes 98312 | tf_op jit(solution)/shard_map/ppermute | solution.py:41
  6.3 7.5 %collective-permute-start = (bf16[16,8,128]{2,1,0:T(8,128)(2,1)}, bf16[16,8,128]{2,1,0:T(8,128)(2,1)S(1)}, u32[]{:S(2)}, u32[]{:S(2)}) collective-permute-start(bf16[16,8,128]{2,1,0:T(8,128)(2,1)} %refs_3_.1), channel_id=1, source_target_pairs={{0,24},{4,28},{8,16},{12,20},{16,8},{20,12},{24,0},{28,4},{1,25},{... | collective-permute-start | bytes 98312 | tf_op jit(solution)/shard_map/ppermute | solution.py:41
  8.8 5.5 %collective-permute-start.1 = (bf16[16,8,128]{2,1,0:T(8,128)(2,1)}, bf16[16,8,128]{2,1,0:T(8,128)(2,1)S(1)}, u32[]{:S(2)}, u32[]{:S(2)}) collective-permute-start(bf16[16,8,128]{2,1,0:T(8,128)(2,1)} %refs_3_.1), channel_id=1, source_target_pairs={{0,16},{4,20},{8,24},{12,28},{16,0},{20,4},{24,8},{28,12},{1,17},{... | collective-permute-start | bytes 98312 | tf_op jit(solution)/shard_map/ppermute | solution.py:41
  9.3 5.0 %collective-permute-start.2 = (bf16[16,8,128]{2,1,0:T(8,128)(2,1)}, bf16[16,8,128]{2,1,0:T(8,128)(2,1)S(1)}, u32[]{:S(2)}, u32[]{:S(2)}) collective-permute-start(bf16[16,8,128]{2,1,0:T(8,128)(2,1)} %refs_3_.1), channel_id=1, source_target_pairs={{0,8},{4,12},{8,0},{12,4},{16,24},{20,28},{24,16},{28,20},{1,9},{5... | collective-permute-start | bytes 98312 | tf_op jit(solution)/shard_map/ppermute | solution.py:41
  10.7 5.6 %collective-permute-start.7 = (bf16[24,16,128]{2,1,0:T(8,128)(2,1)S(1)}, bf16[24,16,128]{2,1,0:T(8,128)(2,1)S(1)}, u32[]{:S(2)}, u32[]{:S(2)}) collective-permute-start(bf16[24,16,128]{2,1,0:T(8,128)(2,1)S(1)} %assemble.3.rest), channel_id=1, source_target_pairs={{0,24},{4,28},{8,16},{12,20},{16,8},{20,12},{24,0},{28,4},{1,25},{... | collective-permute-start | bytes 294920 | tf_op jit(solution)/shard_map/ppermute | solution.py:41
  13.2 4.6 %collective-permute-start.9 = (bf16[24,16,128]{2,1,0:T(8,128)(2,1)S(1)}, bf16[24,16,128]{2,1,0:T(8,128)(2,1)S(1)}, u32[]{:S(2)}, u32[]{:S(2)}) collective-permute-start(bf16[24,16,128]{2,1,0:T(8,128)(2,1)S(1)} %assemble.3.rest), channel_id=1, source_target_pairs={{0,8},{4,12},{8,0},{12,4},{16,24},{20,28},{24,16},{28,20},{1,9},{5... | collective-permute-start | bytes 294920 | tf_op jit(solution)/shard_map/ppermute | solution.py:41
  13.8 4.6 %collective-permute-start.6 = (bf16[24,16,128]{2,1,0:T(8,128)(2,1)S(1)}, bf16[24,16,128]{2,1,0:T(8,128)(2,1)S(1)}, u32[]{:S(2)}, u32[]{:S(2)}) collective-permute-start(bf16[24,16,128]{2,1,0:T(8,128)(2,1)S(1)} %assemble.3.rest), channel_id=1, source_target_pairs={{0,16},{4,20},{8,24},{12,28},{16,0},{20,4},{24,8},{28,12},{1,17},{... | collective-permute-start | bytes 294920 | tf_op jit(solution)/shard_map/ppermute | solution.py:41
  14.4 0.9 %copy-start.1 = (bf16[256,256]{1,0:T(8,128)(2,1)S(1)}, bf16[256,256]{1,0:T(8,128)(2,1)}, u32[]{:S(2)}) copy-start(bf16[256,256]{1,0:T(8,128)(2,1)} %constant.7.clone.refs_1_) | copy-start | bytes 393220
  14.4 0.9 %copy-start.2 = (bf16[128,256]{1,0:T(8,128)(2,1)S(1)}, bf16[128,256]{1,0:T(8,128)(2,1)}, u32[]{:S(2)}) copy-start(bf16[128,256]{1,0:T(8,128)(2,1)} %constant.8.clone.refs_2_) | copy-start | bytes 196612
  14.4 1.0 %copy-start = (bf16[256,256]{1,0:T(8,128)(2,1)S(1)}, bf16[256,256]{1,0:T(8,128)(2,1)}, u32[]{:S(2)}) copy-start(bf16[256,256]{1,0:T(8,128)(2,1)} %constant.6.clone.refs_0_) | copy-start | bytes 393220
  14.4 4.1 %collective-permute-start.11 = (bf16[32,16,128]{2,1,0:T(8,128)(2,1)S(1)}, bf16[32,16,128]{2,1,0:T(8,128)(2,1)S(1)}, u32[]{:S(2)}, u32[]{:S(2)}) collective-permute-start(bf16[32,16,128]{2,1,0:T(8,128)(2,1)S(1)} %join.4.column), channel_id=1, source_target_pairs={{0,4},{4,0},{8,12},{12,8},{16,20},{20,16},{24,28},{28,24},{1,5},{5... | collective-permute-start | bytes 393224 | tf_op jit(solution)/shard_map/ppermute | solution.py:41
  16.4 2.2 %collective-permute-start.12 = (bf16[32,16,128]{2,1,0:T(8,128)(2,1)S(1)}, bf16[32,16,128]{2,1,0:T(8,128)(2,1)S(1)}, u32[]{:S(2)}, u32[]{:S(2)}) collective-permute-start(bf16[32,16,128]{2,1,0:T(8,128)(2,1)S(1)} %join.5), channel_id=1, source_target_pairs={{0,4},{4,0},{8,12},{12,8},{16,20},{20,16},{24,28},{28,24},{1,5},{5... | collective-permute-start | bytes 393224 | tf_op jit(solution)/shard_map/ppermute | solution.py:41
  17.9 2.1 %collective-permute-start.10 = (bf16[32,16,128]{2,1,0:T(8,128)(2,1)S(1)}, bf16[32,16,128]{2,1,0:T(8,128)(2,1)S(1)}, u32[]{:S(2)}, u32[]{:S(2)}) collective-permute-start(bf16[32,16,128]{2,1,0:T(8,128)(2,1)S(1)} %join.7), channel_id=1, source_target_pairs={{0,4},{4,0},{8,12},{12,8},{16,20},{20,16},{24,28},{28,24},{1,5},{5... | collective-permute-start | bytes 393224 | tf_op jit(solution)/shard_map/ppermute | solution.py:41
  18.4 1.6 %collective-permute-start.8 = (bf16[32,16,128]{2,1,0:T(8,128)(2,1)S(1)}, bf16[32,16,128]{2,1,0:T(8,128)(2,1)S(1)}, u32[]{:S(2)}, u32[]{:S(2)}) collective-permute-start(bf16[32,16,128]{2,1,0:T(8,128)(2,1)S(1)} %join.6), channel_id=1, source_target_pairs={{0,4},{4,0},{8,12},{12,8},{16,20},{20,16},{24,28},{28,24},{1,5},{5... | collective-permute-start | bytes 393224 | tf_op jit(solution)/shard_map/ppermute | solution.py:41
